TPU v7x, 512 devices: a whole 4x4x16 slice. The times are simulated.
512 devices in a mesh: tok: 32 (over z_hi, x, core), word: 16 (over y, z_lo).
Axes of the slice: x: 4, y: 4, z: 16 (z_hi: 4, z_lo: 4; z = z_hi * 4 + z_lo), core: 2. Of those that a mesh axis runs over, the one named last changes fastest.
Arguments:
- char_ids: int32 [24, 53248], P(None, 'tok'), may hold values from 0 to 255
- char_table: bfloat16 [256, 16], replicated, may hold values from -6 to 6
- conv_weight: bfloat16 [112, 2048], P(None, 'word'), may hold values from -0.75 to 0.75
- conv_bias: float32 [2048], P('word'), may hold values from -2 to 0
- highway_hid: bfloat16 [2048, 2048], P(None, 'word'), may hold values from -0.125 to 0.125
- highway_gate: bfloat16 [2048, 2048], P(None, 'word'), may hold values from -0.125 to 0.125
- hid_bias: float32 [2048], P('word'), may hold values from -0.5 to 0.5
- gate_bias: float32 [2048], P('word'), may hold values from -2 to 0
- proj_weight: bfloat16 [2048, 1024], P('word'), may hold values from -0.125 to 0.125
- hidden: bfloat16 [8192, 1024], P('tok'), may hold values from -16 to 16
- targets: int32 [8192], replicated, may hold values from 0 to 53247
- counts: int32 [32], replicated, may hold values from 0 to 256, as said below
Outputs:
- embeddings: bfloat16 [53248, 1024], P(('tok', 'word'))
- logprob: float32 [8192], P('tok')
Inputs may be any that keep to these rules, and one draw needn't show every extreme that they name: For every s below 16, counts[s] + counts[s + 16] = 256; some shard holds 256 rows.
All inputs are finite; a program needn't handle non-finite values.
Results may differ from a plain program's by a relative error of at most 0.022.
Values may be sent and summed in bfloat16 or wider, within the bound.
A program may use at most 64 MiB of HBM per device.

v0:
```python
import jax
import jax.numpy as jnp
from jax import lax
from jax.sharding import PartitionSpec as P

CHAR_DIM = 16
KMAX = 7
CHAR_LEN = 24
FILTERS = 2048
TOK_DEV = 256
ROW_BLOCK = 64


lowest_score = -1e30


def filter_mask(first_filter, amount):
    position_row = jnp.arange(KMAX * CHAR_DIM, dtype=jnp.int32) // CHAR_DIM
    filter_index = first_filter + jnp.arange(amount, dtype=jnp.int32)
    filter_width = 1 + filter_index * KMAX // FILTERS
    return position_row[:, None] < filter_width[None, :]


def window_rows(char_table, char_block):
    embedded = jnp.take(char_table, char_block.T, axis=0)
    padded = jnp.pad(embedded, ((0, 0), (0, KMAX - 1), (0, 0)))
    return jnp.concatenate(
        [padded[:, offset_k : offset_k + CHAR_LEN, :] for offset_k in range(KMAX)], axis=2
    )


def char_features(char_ids, char_table, masked, conv_bias):
    word_total = char_ids.shape[1]
    blocks = char_ids.reshape(CHAR_LEN, 8, word_total // 8).transpose(1, 0, 2)

    def conv_block(char_block):
        windows = window_rows(char_table, char_block)
        flat = windows.reshape(-1, KMAX * CHAR_DIM)
        conv = jnp.dot(flat, masked, preferred_element_type=jnp.float32)
        conv = conv.reshape(windows.shape[0], CHAR_LEN, masked.shape[1])
        return jnp.tanh(jnp.max(conv, axis=1) + conv_bias).astype(jnp.bfloat16)

    return lax.map(conv_block, blocks).reshape(word_total, masked.shape[1])


def score_rows(work, work_targets, bound, embeddings, word_at, row_words, span_rows):
    owner = work_targets % row_words // span_rows
    local_col = work_targets // row_words * span_rows + work_targets % span_rows
    wanted = jnp.where(owner == word_at, local_col, -1)
    row_total_count = work.shape[0]
    block_count = (bound + ROW_BLOCK - 1) // ROW_BLOCK
    initial = (
        jnp.full((row_total_count,), lowest_score, jnp.float32),
        jnp.zeros((row_total_count,), jnp.float32),
        jnp.zeros((row_total_count,), jnp.float32),
    )
    portion = lax.all_gather(embeddings, "tok", axis=0, tiled=True)
    columns = jnp.arange(portion.shape[0], dtype=jnp.int32)

    def one_block(block_id, state):
        row_best, row_total, row_pick = state
        first_row = block_id * ROW_BLOCK
        queries = lax.dynamic_slice_in_dim(work, first_row, ROW_BLOCK, 0)
        scores = lax.dot_general(
            queries, portion, (((1,), (1,)), ((), ())), preferred_element_type=jnp.float32
        )
        old_best = lax.dynamic_slice_in_dim(row_best, first_row, ROW_BLOCK)
        old_total = lax.dynamic_slice_in_dim(row_total, first_row, ROW_BLOCK)
        old_pick = lax.dynamic_slice_in_dim(row_pick, first_row, ROW_BLOCK)
        new_best = jnp.maximum(old_best, jnp.max(scores, axis=1))
        new_total = old_total * jnp.exp(old_best - new_best) + jnp.sum(
            jnp.exp(scores - new_best[:, None]), axis=1
        )
        hits = lax.dynamic_slice_in_dim(wanted, first_row, ROW_BLOCK)[:, None] == columns[None, :]
        new_pick = old_pick + jnp.sum(jnp.where(hits, scores, 0.0), axis=1)
        return (
            lax.dynamic_update_slice_in_dim(row_best, new_best, first_row, 0),
            lax.dynamic_update_slice_in_dim(row_total, new_total, first_row, 0),
            lax.dynamic_update_slice_in_dim(row_pick, new_pick, first_row, 0),
        )

    row_best, row_total, row_pick = lax.fori_loop(0, block_count, one_block, initial)
    top_score = lax.pmax(row_best, "word")
    summed, picked = lax.psum((row_total * jnp.exp(row_best - top_score), row_pick), "word")
    labelled = jnp.arange(row_total_count, dtype=jnp.int32) < bound
    safe_total = jnp.where(labelled, summed, 1.0)
    return jnp.where(labelled, picked - top_score - jnp.log(safe_total), 0.0)


def on_device(
    char_ids,
    char_table,
    conv_weight,
    conv_bias,
    highway_hid,
    highway_gate,
    hid_bias,
    gate_bias,
    proj_weight,
    hidden,
    targets,
    counts,
):
    word_at = lax.axis_index("word")
    tok_at = lax.axis_index("tok")
    word_size = lax.axis_size("word")
    filt_dev = conv_weight.shape[1]
    masked = conv_weight * filter_mask(word_at * filt_dev, filt_dev).astype(jnp.bfloat16)
    feats = char_features(char_ids, char_table, masked, conv_bias)
    row_words = feats.shape[0]
    weights_both = jnp.concatenate([highway_hid, highway_gate], axis=1)
    mixed = jnp.dot(
        lax.all_gather(feats, "word", axis=1, tiled=True),
        weights_both,
        preferred_element_type=jnp.float32,
    )
    hid_in = mixed[:, :filt_dev] + hid_bias
    gate_in = mixed[:, filt_dev:] + gate_bias
    opened = jax.nn.sigmoid(gate_in)
    highway = (opened * jax.nn.relu(hid_in) + (1.0 - opened) * feats.astype(jnp.float32)).astype(
        jnp.bfloat16
    )
    span_rows = row_words // word_size
    embeddings = lax.psum_scatter(
        jnp.dot(highway, proj_weight, preferred_element_type=jnp.float32).astype(jnp.bfloat16),
        "word",
        scatter_dimension=0,
        tiled=True,
    )
    own_count = lax.dynamic_index_in_dim(counts, tok_at, keepdims=False)
    own_targets = lax.dynamic_slice_in_dim(targets, tok_at * TOK_DEV, TOK_DEV)
    logprob = score_rows(hidden, own_targets, own_count, embeddings, word_at, row_words, span_rows)
    return (embeddings, logprob)


def solution(mesh):
    return jax.shard_map(
        on_device,
        mesh=mesh,
        in_specs=(
            P(None, "tok"),
            P(),
            P(None, "word"),
            P("word"),
            P(None, "word"),
            P(None, "word"),
            P("word"),
            P("word"),
            P("word", None),
            P("tok", None),
            P(),
            P(),
        ),
        out_specs=(P(("tok", "word"), None), P("tok")),
        check_vma=False,
    )
```

profile of v0, /device:TPU:2, one launch (start us, length us, event | category | flops | bytes accessed | tf_op | source)
XLA Modules:
  0.0 738.3 jit_solution(18135260197498879622)
XLA Ops:
  7.2 2.2 copy.16
  10.3 0.8 compare_select_fusion.1
  11.1 214.5 %while.27 = (s32[]{:T(128)}, bf16[8,208,128]{2,1,0:T(8,128)(2,1)S(1)}, s32[8,24,208]{1,2,0:T(8,128)}, bf16[256,16]{1,0:T(8,128)(2,1)S(1)}, bf16[112,128]{1,0:T(8,128)(2,1)S(1)}, /*index=5*/f32[128]{0:T(128)}, s32[]{:T(128)}) while((s32[]{:T(128)}, bf16[8,208,128]{2,1,0:T(8,128)(2,1)S(1)}, s32[8,24,208]{1,2,0:T(8,128)}, ...), condition=%wide.region_2.3_spmd, body=%wide.region_0.2_spmd.sunk | while | flops 143911168 | bytes 5559673 | solution.py:43
  11.1 0.9 compare_and_fusion.2
  12.2 10.0 %gather_fusion = bf16[4992,16]{1,0:T(8,128)(2,1)S(1)} fusion(bf16[256,16]{1,0:T(8,128)(2,1)S(1)} %get-tuple-element.346, s32[5120]{0:T(1024)S(1)} %pad_clamp_fusion.2), kind=kCustom, calls=%fused_computation.clone.1 | custom fusion | bytes 339456 | tf_op jit(solution)/shard_map/while/body/eval_jaxpr/jit(_take)/gather | solution.py:25
  22.2 1.0 broadcast_select_fusion.2
  23.2 3.5 pad_slice_fusion.7
  26.7 9.0 %concatenate.11 = bf16[208,24,112]{2,1,0:T(8,128)(2,1)} concatenate(bf16[208,24,16]{2,1,0:T(8,128)(2,1)S(1)} %broadcast_select_fusion.2, bf16[208,24,16]{2,1,0:T(8,128)(2,1)} %get-tuple-element.307, bf16[208,24,16]{2,1,0:T(8,128)(2,1)} %get-tuple-element.308, bf16[208,24,16]{2,1,0:T(8,128)(2,1)} %get-tuple-element.309, bf16[208,24,16]{2,1,0:T(8,128)(2,1)} %get-tuple-element.310, ...), dimensions={2} | concatenate | bytes 2236416 | tf_op jit(solution)/shard_map/while/body/eval_jaxpr/concatenate | solution.py:27
  35.7 2.1 convolution_reduce_fusion.2
  37.9 0.9 compare_and_fusion.2
  39.0 10.0 %gather_fusion = bf16[4992,16]{1,0:T(8,128)(2,1)S(1)} fusion(bf16[256,16]{1,0:T(8,128)(2,1)S(1)} %get-tuple-element.346, s32[5120]{0:T(1024)S(1)} %pad_clamp_fusion.2), kind=kCustom, calls=%fused_computation.clone.1 | custom fusion | bytes 339456 | tf_op jit(solution)/shard_map/while/body/eval_jaxpr/jit(_take)/gather | solution.py:25
  49.0 1.0 broadcast_select_fusion.2
  50.0 3.5 pad_slice_fusion.7
  53.5 9.0 %concatenate.11 = bf16[208,24,112]{2,1,0:T(8,128)(2,1)} concatenate(bf16[208,24,16]{2,1,0:T(8,128)(2,1)S(1)} %broadcast_select_fusion.2, bf16[208,24,16]{2,1,0:T(8,128)(2,1)} %get-tuple-element.307, bf16[208,24,16]{2,1,0:T(8,128)(2,1)} %get-tuple-element.308, bf16[208,24,16]{2,1,0:T(8,128)(2,1)} %get-tuple-element.309, bf16[208,24,16]{2,1,0:T(8,128)(2,1)} %get-tuple-element.310, ...), dimensions={2} | concatenate | bytes 2236416 | tf_op jit(solution)/shard_map/while/body/eval_jaxpr/concatenate | solution.py:27
  62.5 2.1 convolution_reduce_fusion.2
  64.7 0.9 compare_and_fusion.2
  65.8 10.0 %gather_fusion = bf16[4992,16]{1,0:T(8,128)(2,1)S(1)} fusion(bf16[256,16]{1,0:T(8,128)(2,1)S(1)} %get-tuple-element.346, s32[5120]{0:T(1024)S(1)} %pad_clamp_fusion.2), kind=kCustom, calls=%fused_computation.clone.1 | custom fusion | bytes 339456 | tf_op jit(solution)/shard_map/while/body/eval_jaxpr/jit(_take)/gather | solution.py:25
  75.8 1.0 broadcast_select_fusion.2
  76.8 3.5 pad_slice_fusion.7
  80.3 9.0 %concatenate.11 = bf16[208,24,112]{2,1,0:T(8,128)(2,1)} concatenate(bf16[208,24,16]{2,1,0:T(8,128)(2,1)S(1)} %broadcast_select_fusion.2, bf16[208,24,16]{2,1,0:T(8,128)(2,1)} %get-tuple-element.307, bf16[208,24,16]{2,1,0:T(8,128)(2,1)} %get-tuple-element.308, bf16[208,24,16]{2,1,0:T(8,128)(2,1)} %get-tuple-element.309, bf16[208,24,16]{2,1,0:T(8,128)(2,1)} %get-tuple-element.310, ...), dimensions={2} | concatenate | bytes 2236416 | tf_op jit(solution)/shard_map/while/body/eval_jaxpr/concatenate | solution.py:27
  89.3 2.1 convolution_reduce_fusion.2
  91.5 0.9 compare_and_fusion.2
  92.6 10.0 %gather_fusion = bf16[4992,16]{1,0:T(8,128)(2,1)S(1)} fusion(bf16[256,16]{1,0:T(8,128)(2,1)S(1)} %get-tuple-element.346, s32[5120]{0:T(1024)S(1)} %pad_clamp_fusion.2), kind=kCustom, calls=%fused_computation.clone.1 | custom fusion | bytes 339456 | tf_op jit(solution)/shard_map/while/body/eval_jaxpr/jit(_take)/gather | solution.py:25
  102.6 1.0 broadcast_select_fusion.2
  103.6 3.5 pad_slice_fusion.7
  107.1 9.0 %concatenate.11 = bf16[208,24,112]{2,1,0:T(8,128)(2,1)} concatenate(bf16[208,24,16]{2,1,0:T(8,128)(2,1)S(1)} %broadcast_select_fusion.2, bf16[208,24,16]{2,1,0:T(8,128)(2,1)} %get-tuple-element.307, bf16[208,24,16]{2,1,0:T(8,128)(2,1)} %get-tuple-element.308, bf16[208,24,16]{2,1,0:T(8,128)(2,1)} %get-tuple-element.309, bf16[208,24,16]{2,1,0:T(8,128)(2,1)} %get-tuple-element.310, ...), dimensions={2} | concatenate | bytes 2236416 | tf_op jit(solution)/shard_map/while/body/eval_jaxpr/concatenate | solution.py:27
  116.1 2.1 convolution_reduce_fusion.2
  118.3 0.9 compare_and_fusion.2
  119.4 10.0 %gather_fusion = bf16[4992,16]{1,0:T(8,128)(2,1)S(1)} fusion(bf16[256,16]{1,0:T(8,128)(2,1)S(1)} %get-tuple-element.346, s32[5120]{0:T(1024)S(1)} %pad_clamp_fusion.2), kind=kCustom, calls=%fused_computation.clone.1 | custom fusion | bytes 339456 | tf_op jit(solution)/shard_map/while/body/eval_jaxpr/jit(_take)/gather | solution.py:25
  129.4 1.0 broadcast_select_fusion.2
  130.4 3.5 pad_slice_fusion.7
  133.9 9.0 %concatenate.11 = bf16[208,24,112]{2,1,0:T(8,128)(2,1)} concatenate(bf16[208,24,16]{2,1,0:T(8,128)(2,1)S(1)} %broadcast_select_fusion.2, bf16[208,24,16]{2,1,0:T(8,128)(2,1)} %get-tuple-element.307, bf16[208,24,16]{2,1,0:T(8,128)(2,1)} %get-tuple-element.308, bf16[208,24,16]{2,1,0:T(8,128)(2,1)} %get-tuple-element.309, bf16[208,24,16]{2,1,0:T(8,128)(2,1)} %get-tuple-element.310, ...), dimensions={2} | concatenate | bytes 2236416 | tf_op jit(solution)/shard_map/while/body/eval_jaxpr/concatenate | solution.py:27
  142.9 2.1 convolution_reduce_fusion.2
  145.2 0.9 compare_and_fusion.2
  146.2 10.0 %gather_fusion = bf16[4992,16]{1,0:T(8,128)(2,1)S(1)} fusion(bf16[256,16]{1,0:T(8,128)(2,1)S(1)} %get-tuple-element.346, s32[5120]{0:T(1024)S(1)} %pad_clamp_fusion.2), kind=kCustom, calls=%fused_computation.clone.1 | custom fusion | bytes 339456 | tf_op jit(solution)/shard_map/while/body/eval_jaxpr/jit(_take)/gather | solution.py:25
  156.2 1.0 broadcast_select_fusion.2
  157.2 3.5 pad_slice_fusion.7
  160.7 9.0 %concatenate.11 = bf16[208,24,112]{2,1,0:T(8,128)(2,1)} concatenate(bf16[208,24,16]{2,1,0:T(8,128)(2,1)S(1)} %broadcast_select_fusion.2, bf16[208,24,16]{2,1,0:T(8,128)(2,1)} %get-tuple-element.307, bf16[208,24,16]{2,1,0:T(8,128)(2,1)} %get-tuple-element.308, bf16[208,24,16]{2,1,0:T(8,128)(2,1)} %get-tuple-element.309, bf16[208,24,16]{2,1,0:T(8,128)(2,1)} %get-tuple-element.310, ...), dimensions={2} | concatenate | bytes 2236416 | tf_op jit(solution)/shard_map/while/body/eval_jaxpr/concatenate | solution.py:27
  169.7 2.1 convolution_reduce_fusion.2
  172.0 0.9 compare_and_fusion.2
  173.0 10.0 %gather_fusion = bf16[4992,16]{1,0:T(8,128)(2,1)S(1)} fusion(bf16[256,16]{1,0:T(8,128)(2,1)S(1)} %get-tuple-element.346, s32[5120]{0:T(1024)S(1)} %pad_clamp_fusion.2), kind=kCustom, calls=%fused_computation.clone.1 | custom fusion | bytes 339456 | tf_op jit(solution)/shard_map/while/body/eval_jaxpr/jit(_take)/gather | solution.py:25
  183.0 1.0 broadcast_select_fusion.2
  184.0 3.5 pad_slice_fusion.7
  187.5 9.0 %concatenate.11 = bf16[208,24,112]{2,1,0:T(8,128)(2,1)} concatenate(bf16[208,24,16]{2,1,0:T(8,128)(2,1)S(1)} %broadcast_select_fusion.2, bf16[208,24,16]{2,1,0:T(8,128)(2,1)} %get-tuple-element.307, bf16[208,24,16]{2,1,0:T(8,128)(2,1)} %get-tuple-element.308, bf16[208,24,16]{2,1,0:T(8,128)(2,1)} %get-tuple-element.309, bf16[208,24,16]{2,1,0:T(8,128)(2,1)} %get-tuple-element.310, ...), dimensions={2} | concatenate | bytes 2236416 | tf_op jit(solution)/shard_map/while/body/eval_jaxpr/concatenate | solution.py:27
  196.6 2.1 convolution_reduce_fusion.2
  198.8 0.9 compare_and_fusion.2
  199.8 10.0 %gather_fusion = bf16[4992,16]{1,0:T(8,128)(2,1)S(1)} fusion(bf16[256,16]{1,0:T(8,128)(2,1)S(1)} %get-tuple-element.346, s32[5120]{0:T(1024)S(1)} %pad_clamp_fusion.2), kind=kCustom, calls=%fused_computation.clone.1 | custom fusion | bytes 339456 | tf_op jit(solution)/shard_map/while/body/eval_jaxpr/jit(_take)/gather | solution.py:25
  209.8 1.0 broadcast_select_fusion.2
  210.9 3.5 pad_slice_fusion.7
  214.3 9.0 %concatenate.11 = bf16[208,24,112]{2,1,0:T(8,128)(2,1)} concatenate(bf16[208,24,16]{2,1,0:T(8,128)(2,1)S(1)} %broadcast_select_fusion.2, bf16[208,24,16]{2,1,0:T(8,128)(2,1)} %get-tuple-element.307, bf16[208,24,16]{2,1,0:T(8,128)(2,1)} %get-tuple-element.308, bf16[208,24,16]{2,1,0:T(8,128)(2,1)} %get-tuple-element.309, bf16[208,24,16]{2,1,0:T(8,128)(2,1)} %get-tuple-element.310, ...), dimensions={2} | concatenate | bytes 2236416 | tf_op jit(solution)/shard_map/while/body/eval_jaxpr/concatenate | solution.py:27
  223.4 2.1 convolution_reduce_fusion.2
  226.5 168.1 %all-gather.3.cloned.1.call-done = bf16[1664,2048]{1,0:T(8,128)(2,1)} async-done(((bf16[1664,128]{1,0:T(8,128)(2,1)}), bf16[1664,2048]{1,0:T(8,128)(2,1)}) %all-gather.3.cloned.1.call-update) | async-done | bytes 6815760 | tf_op jit(solution)/shard_map/all_gather | solution.py:113
  394.6 5.2 fusion.9
  399.8 2.8 convolution_convert_fusion
  402.7 101.3 %reduce-scatter.2.cloned.1.call-done = bf16[104,1024]{1,0:T(8,128)(2,1)} async-done(((bf16[1664,1024]{1,0:T(8,128)(2,1)}), bf16[104,1024]{1,0:T(8,128)(2,1)}) %reduce-scatter.2.cloned.1.call-update) | async-done | bytes 213008 | tf_op jit(solution)/shard_map/reduce_scatter | solution.py:124
  506.0 119.4 %all-gather.5.cloned.1.call-done = bf16[3328,1024]{1,0:T(8,128)(2,1)} async-done(((bf16[104,1024]{1,0:T(8,128)(2,1)}), bf16[3328,1024]{1,0:T(8,128)(2,1)}) %all-gather.5.cloned.1.call-update) | async-done | bytes 6815760 | tf_op jit(solution)/shard_map/all_gather | solution.py:57
  625.4 24.5 %while.28 = (s32[]{:T(128)}, f32[256]{0:T(256)S(1)}, f32[256]{0:T(256)S(1)}, f32[256]{0:T(256)S(1)}, s32[]{:T(128)}, /*index=5*/bf16[256,1024]{1,0:T(8,128)(2,1)...) while((s32[]{:T(128)}, f32[256]{0:T(256)S(1)}, ...), condition=%wide.region_8.9_spmd.clone, body=%wide.region_4.8_spmd.clone.sunk | while | flops 437485696 | bytes 8662971 | solution.py:82
  625.4 5.3 fusion.47
  631.5 5.3 fusion.47
  637.7 5.3 fusion.47
  643.8 5.3 fusion.47
  649.9 42.7 %pmax.7 = f32[256]{0:T(256)S(1)} all-reduce(f32[256]{0:T(256)S(1)} %get-tuple-element.131), channel_id=1, replica_groups=mesh['tok'=32,'word'=16] {'word'}, use_global_device_ids=true, to_apply=%region_10.11 | all-reduce | flops 256 | bytes 2048 | tf_op jit(solution)/shard_map/pmax | solution.py:83
  692.7 38.0 %all-reduce.1 = (f32[256]{0:T(256)S(1)}, f32[256]{0:T(256)S(1)}) all-reduce(f32[256]{0:T(256)S(1)} %exponential_multiply_fusion, f32[256]{0:T(256)S(1)} %get-tuple-element.130), channel_id=1, replica_groups=mesh['tok'=32,'word'=16] {'word'}, use_global_device_ids=true, to_apply=%region_11.12 | all-reduce | flops 512 | bytes 4096 | tf_op jit(solution)/shard_map/psum | solution.py:84
  730.6 1.2 subtract_select_fusion
  (92 shorter events, 7.7 us)
Async XLA Ops:
  7.2 392.6 %copy-start = (bf16[128,1024]{1,0:T(8,128)(2,1)S(1)}, bf16[128,1024]{1,0:T(8,128)(2,1)}, u32[]{:S(2)}) copy-start(bf16[128,1024]{1,0:T(8,128)(2,1)} %param.24) | copy-start | bytes 786436
  7.2 387.4 %all-gather.3.cloned.1.call-start = ((), (), s32[]{:S(2)}) async-start(), calls=%async_computation.1 | async-start | bytes 7241728 | tf_op jit(solution)/shard_map/all_gather | solution.py:113
  26.7 11.2 %copy-start.3 = (f32[128]{0:T(128)S(1)}, f32[128]{0:T(128)}, u32[]{:S(2)}) copy-start(f32[128]{0:T(128)} %get-tuple-element.348) | copy-start | bytes 1540 | tf_op jit(solution)/shard_map/while
  53.5 11.2 %copy-start.3 = (f32[128]{0:T(128)S(1)}, f32[128]{0:T(128)}, u32[]{:S(2)}) copy-start(f32[128]{0:T(128)} %get-tuple-element.348) | copy-start | bytes 1540 | tf_op jit(solution)/shard_map/while
  80.3 11.2 %copy-start.3 = (f32[128]{0:T(128)S(1)}, f32[128]{0:T(128)}, u32[]{:S(2)}) copy-start(f32[128]{0:T(128)} %get-tuple-element.348) | copy-start | bytes 1540 | tf_op jit(solution)/shard_map/while
  107.1 11.2 %copy-start.3 = (f32[128]{0:T(128)S(1)}, f32[128]{0:T(128)}, u32[]{:S(2)}) copy-start(f32[128]{0:T(128)} %get-tuple-element.348) | copy-start | bytes 1540 | tf_op jit(solution)/shard_map/while
  133.9 11.2 %copy-start.3 = (f32[128]{0:T(128)S(1)}, f32[128]{0:T(128)}, u32[]{:S(2)}) copy-start(f32[128]{0:T(128)} %get-tuple-element.348) | copy-start | bytes 1540 | tf_op jit(solution)/shard_map/while
  160.7 11.2 %copy-start.3 = (f32[128]{0:T(128)S(1)}, f32[128]{0:T(128)}, u32[]{:S(2)}) copy-start(f32[128]{0:T(128)} %get-tuple-element.348) | copy-start | bytes 1540 | tf_op jit(solution)/shard_map/while
  187.5 11.2 %copy-start.3 = (f32[128]{0:T(128)S(1)}, f32[128]{0:T(128)}, u32[]{:S(2)}) copy-start(f32[128]{0:T(128)} %get-tuple-element.348) | copy-start | bytes 1540 | tf_op jit(solution)/shard_map/while
  214.3 11.2 %copy-start.3 = (f32[128]{0:T(128)S(1)}, f32[128]{0:T(128)}, u32[]{:S(2)}) copy-start(f32[128]{0:T(128)} %get-tuple-element.348) | copy-start | bytes 1540 | tf_op jit(solution)/shard_map/while
  225.6 0.8 copy-start.1
  226.4 173.4 %copy-start.2 = (bf16[8,208,128]{2,1,0:T(8,128)(2,1)S(1)}, bf16[8,208,128]{2,1,0:T(8,128)(2,1)}, u32[]{:S(2)}) copy-start(bf16[8,208,128]{2,1,0:T(8,128)(2,1)} %copy-done.1) | copy-start | bytes 1277956
  226.4 173.4 %copy-start.4 = (f32[128]{0:T(128)S(1)}, f32[128]{0:T(128)}, u32[]{:S(2)}) copy-start(f32[128]{0:T(128)} %param.22) | copy-start | bytes 1540
  226.4 173.4 %copy-start.5 = (f32[128]{0:T(128)S(1)}, f32[128]{0:T(128)}, u32[]{:S(2)}) copy-start(f32[128]{0:T(128)} %param.23) | copy-start | bytes 1540
  226.4 277.5 %reduce-scatter.2.cloned.1.call-start = ((), (), s32[]{:S(2)}) async-start(), calls=%async_computation.2 | async-start | bytes 3620864 | tf_op jit(solution)/shard_map/reduce_scatter | solution.py:124
  402.6 101.4 %copy-start.6 = (s32[32]{0:T(128)S(1)}, s32[32]{0:T(128)}, u32[]{:S(2)}) copy-start(s32[32]{0:T(128)} %param.27) | copy-start | bytes 388
  402.6 222.8 %all-gather.5.cloned.1.call-start = ((), (), s32[]{:S(2)}) async-start(), calls=%async_computation.3 | async-start | bytes 7028736 | tf_op jit(solution)/shard_map/all_gather | solution.py:57
Sparse Core Ops, SparseCore 0:
  226.5 168.0 all-gather.2
  402.7 101.1 reduce-scatter.1
  508.1 117.2 all-gather.4
where the time goes:
time: 741 us; the launch traced here: 738 us
  waiting for transfers between devices  389 us (52%)
  local copies, waits for them, and re-layouts  186 us (25%)
  blocking collectives  80.7 us (11%)
  matrix products  46.3 us (6%)
  other arithmetic  21.9 us (3%)
  between operations  14.5 us (2%)
    all_gather x1, waiting for transfers between devices, on_device(): lax.all_gather(feats, 'word', axis=1, tiled=True)  168 us
    all_gather x1, waiting for transfers between devices, score_rows(): portion = lax.all_gather(embeddings, 'tok', axis=0, tiled=True)  119 us
    reduce_scatter x1, waiting for transfers between devices, on_device(): lax.psum_scatter(jnp.dot(highway, proj_weight, preferred_element_type=jnp...  101 us
    gather x8, local copies, waits for them, and re-layouts, window_rows(): embedded = jnp.take(char_table, char_block.T, axis=0)  79.8 us
    concatenate x8, local copies, waits for them, and re-layouts, window_rows(): jnp.concatenate([padded[:, offset_k:offset_k + CHAR_LEN, :] for offset_k...  72.4 us
    pmax x1, blocking collectives, score_rows(): top_score = lax.pmax(row_best, 'word')  42.7 us
    psum x1, blocking collectives, score_rows(): lax.psum((row_total * jnp.exp(row_best - top_score), row_pick), 'word')  38 us
    slice x8, local copies, waits for them, and re-layouts, window_rows(): padded[:, offset_k:offset_k + CHAR_LEN, :]  27.7 us
  transfers between devices with their start and end apart: 3, of which 3 were waited for; matrix products, arithmetic and copies ran while one was open for 0% of the time, Pallas kernels for 0%

commit v1 on v0

--- a/solution.py
+++ b/solution.py
@@ -1,6 +1,10 @@
+import functools
+
 import jax
 import jax.numpy as jnp
 from jax import lax
+from jax.experimental import pallas as pl
+from jax.experimental.pallas import tpu as pltpu
 from jax.sharding import PartitionSpec as P
 
 CHAR_DIM = 16
@@ -9,38 +13,210 @@
 FILTERS = 2048
 TOK_DEV = 256
 ROW_BLOCK = 64
+MESH = pl.DeviceIdType.MESH
+BF16 = jnp.bfloat16
+F32 = jnp.float32
+
+GROUP = 4
+OWN = 104
+BLOCK = GROUP * OWN
+SLICE = 128
+WIDE = GROUP * SLICE
+PACK = 2560
+CHUNK = PACK // 8
 
 
 lowest_score = -1e30
 
 
-def filter_mask(first_filter, amount):
-    position_row = jnp.arange(KMAX * CHAR_DIM, dtype=jnp.int32) // CHAR_DIM
-    filter_index = first_filter + jnp.arange(amount, dtype=jnp.int32)
-    filter_width = 1 + filter_index * KMAX // FILTERS
-    return position_row[:, None] < filter_width[None, :]
-
-
-def window_rows(char_table, char_block):
-    embedded = jnp.take(char_table, char_block.T, axis=0)
-    padded = jnp.pad(embedded, ((0, 0), (0, KMAX - 1), (0, 0)))
-    return jnp.concatenate(
-        [padded[:, offset_k : offset_k + CHAR_LEN, :] for offset_k in range(KMAX)], axis=2
+def dot(a, b):
+    return jnp.dot(a, b, preferred_element_type=F32)
+
+
+def embed_kernel(
+    ids_ref, table_ref, conv_ref, cbias_ref, hid_ref, gate_ref, hbias_ref, gbias_ref, proj_ref,
+    out_ref,
+    weights, convs, biases, tables, chars, shifted, best, feats, highway, parts, arrived,
+    send_sem, recv_sem,
+):
+    tok, word = lax.axis_index("tok"), lax.axis_index("word")
+    zhi, x, core = tok // 8, (tok // 2) % 4, tok % 2
+    y, zlo = word // 4, word % 4
+
+    def at(x_to=x, core_to=core, y_to=y, zlo_to=zlo):
+        return (zhi * 8 + x_to * 2 + core_to, y_to * 4 + zlo_to)
+
+    def copy(number, src, dst, to):
+        return pltpu.make_async_remote_copy(
+            src_ref=src, dst_ref=dst, send_sem=send_sem.at[number], recv_sem=recv_sem.at[number],
+            device_id=to, device_id_type=MESH,
+        )
+
+    barrier = pltpu.get_barrier_semaphore()
+    partners = [at(core_to=core ^ 1)]
+    for d in (1, 2, 3):
+        partners += [at(zlo_to=zlo ^ d), at(x_to=x ^ d), at(y_to=y ^ d)]
+    for partner in partners:
+        pl.semaphore_signal(barrier, inc=1, device_id=partner, device_id_type=MESH)
+
+    convs[zlo] = conv_ref[...]
+    biases[zlo, 0:1, :] = cbias_ref[...]
+    biases[zlo, 1:2, :] = hbias_ref[...]
+    biases[zlo, 2:3, :] = gbias_ref[...]
+    weights[zlo, 0:2048, 0:128] = hid_ref[...]
+    weights[zlo, 0:2048, 128:256] = gate_ref[...]
+    for cb in range(4):
+        weights[zlo, 2048 + cb * 128 : 2176 + cb * 128, :] = proj_ref[:, cb * 256 : cb * 256 + 256]
+
+    pl.semaphore_wait(barrier, len(partners))
+
+    sends = []
+
+    def start(number, src, dst, to):
+        c = copy(number, src, dst, to)
+        c.start()
+        sends.append(c)
+
+    mine = pl.ds(pl.multiple_of((core * 4 + x) * CHUNK, CHUNK), CHUNK)
+    core_rows = pl.ds(pl.multiple_of(core * 4 * CHUNK, CHUNK), 4 * CHUNK)
+    other_rows = pl.ds(pl.multiple_of((core ^ 1) * 4 * CHUNK, CHUNK), 4 * CHUNK)
+    for d in (1, 2, 3):
+        to = at(zlo_to=zlo ^ d)
+        start(d - 1, convs.at[zlo], convs.at[zlo], to)
+        start(2 + d, biases.at[zlo], biases.at[zlo], to)
+    for d in (1, 2, 3):
+        start(5 + d, weights.at[zlo, mine], weights.at[zlo, mine], at(zlo_to=zlo ^ d))
+
+    row = lax.broadcasted_iota(jnp.int32, (BLOCK, GROUP * BLOCK), 0)
+    column = lax.broadcasted_iota(jnp.int32, (BLOCK, GROUP * BLOCK), 1)
+    source = row + (row // OWN) * (BLOCK - OWN) + zlo * OWN
+    chosen = (source == column).astype(F32).astype(BF16)
+    spelled = lax.dot_general(
+        chosen, ids_ref[...].astype(F32).astype(BF16), (((1,), (1,)), ((), ())),
+        preferred_element_type=F32,
+    ).astype(jnp.int32)
+    letter = lax.broadcasted_iota(jnp.int32, (BLOCK, 256), 1)
+    place_row = lax.broadcasted_iota(jnp.int32, (CHAR_DIM, 128), 0)
+    place_col = lax.broadcasted_iota(jnp.int32, (CHAR_DIM, 128), 1)
+    for j in range(8):
+        place = (place_col == place_row + CHAR_DIM * j).astype(F32).astype(BF16)
+        tables[j] = dot(table_ref[...], place).astype(BF16)
+    for i in range(3):
+        total = jnp.zeros((BLOCK, 128), F32)
+        for j in range(8):
+            p = 8 * i + j
+            hot = (spelled[:, p : p + 1] == letter).astype(F32).astype(BF16)
+            total += dot(hot, tables[j])
+        chars[:, 128 * i : 128 * i + 128] = total.astype(BF16)
+    chars[:, 384:512] = jnp.zeros((BLOCK, 128), BF16)
+
+    for d in (1, 2, 3):
+        copy(d - 1, convs.at[zlo ^ d], convs.at[zlo ^ d], at(zlo_to=zlo ^ d)).wait_recv()
+        copy(2 + d, biases.at[zlo ^ d], biases.at[zlo ^ d], at(zlo_to=zlo ^ d)).wait_recv()
+    tap = lax.broadcasted_iota(jnp.int32, (KMAX * CHAR_DIM, WIDE), 0) // CHAR_DIM
+    number = y * WIDE + lax.broadcasted_iota(jnp.int32, (KMAX * CHAR_DIM, WIDE), 1)
+    keep = tap < 1 + number * KMAX // FILTERS
+    filters = jnp.concatenate([convs[q] for q in range(GROUP)], axis=1).astype(F32)
+    filters = jnp.where(keep, filters, 0.0).astype(BF16)
+    for j in range(8):
+        shifted[j] = jnp.zeros((256, WIDE), BF16)
+        shifted[j, CHAR_DIM * j : CHAR_DIM * (j + KMAX), :] = filters
+    best[...] = jnp.full((BLOCK, WIDE), -3e38, F32)
+
+    def conv_step(j, carry):
+        taps = shifted[j]
+        top = dot(chars[:, 0:256], taps)
+        top = jnp.maximum(top, dot(chars[:, 128:384], taps))
+        top = jnp.maximum(top, dot(chars[:, 256:512], taps))
+        best[...] = jnp.maximum(best[...], top)
+        return carry
+
+    lax.fori_loop(0, 8, conv_step, 0)
+    bias = jnp.concatenate([biases[q, 0:1, :] for q in range(GROUP)], axis=1)
+    feats[y] = jnp.tanh(best[...] + bias).astype(BF16)
+    for d in (1, 2, 3):
+        start(8 + d, feats.at[y], feats.at[y], at(y_to=y ^ d))
+
+    for d in (1, 2, 3):
+        q = zlo ^ d
+        copy(5 + d, weights.at[q, mine], weights.at[q, mine], at(zlo_to=q)).wait_recv()
+        for k in (1, 2, 3):
+            start(12 + (d - 1) * 3 + k - 1, weights.at[q, mine], weights.at[q, mine], at(x_to=x ^ k))
+    for d in (1, 2, 3):
+        q = zlo ^ d
+        for k in (1, 2, 3):
+            theirs = pl.ds(pl.multiple_of((core * 4 + (x ^ k)) * CHUNK, CHUNK), CHUNK)
+            copy(
+                12 + (d - 1) * 3 + k - 1, weights.at[q, theirs], weights.at[q, theirs], at(x_to=x ^ k)
+            ).wait_recv()
+        start(20 + d, weights.at[q, core_rows], weights.at[q, core_rows], at(core_to=core ^ 1))
+    for d in (1, 2, 3):
+        q = zlo ^ d
+        copy(20 + d, weights.at[q, other_rows], weights.at[q, other_rows], at(core_to=core ^ 1)).wait_recv()
+    for d in (1, 2, 3):
+        copy(8 + d, feats.at[y ^ d], feats.at[y ^ d], at(y_to=y ^ d)).wait_recv()
+
+    for q in range(GROUP):
+        mixed = dot(feats[0], weights[q, 0:512, :])
+        for g in range(1, GROUP):
+            mixed += dot(feats[g], weights[q, 512 * g : 512 * g + 512, :])
+        hid_in = mixed[:, :128] + biases[q, 1:2, :]
+        gate_in = mixed[:, 128:] + biases[q, 2:3, :]
+        opened = jax.nn.sigmoid(gate_in)
+        carried = feats[y, :, 128 * q : 128 * q + 128].astype(F32)
+        highway[:, 128 * q : 128 * q + 128] = (
+            opened * jnp.maximum(hid_in, 0.0) + (1.0 - opened) * carried
+        ).astype(BF16)
+
+    for cb in range(4):
+        matrix = jnp.concatenate(
+            [weights[q, 2048 + cb * 128 : 2176 + cb * 128, :] for q in range(GROUP)], axis=0
+        )
+        product = dot(highway[...], matrix)
+        for g in range(GROUP):
+            parts[g, :, cb * 256 : cb * 256 + 256] = product[g * OWN : g * OWN + OWN, :].astype(BF16)
+    for d in (1, 2, 3):
+        start(23 + d, parts.at[y ^ d], arrived.at[d - 1], at(y_to=y ^ d))
+    total = parts[y].astype(F32)
+    for d in (1, 2, 3):
+        copy(23 + d, parts.at[y], arrived.at[d - 1], at(y_to=y ^ d)).wait_recv()
+        total += arrived[d - 1].astype(F32)
+    out_ref[...] = total.astype(BF16)
+    for c in sends:
+        c.wait_send()
+
+
+def build_embeddings(char_ids, char_table, conv_weight, conv_bias, hid, gate, hid_bias, gate_bias, proj):
+    vmem = pl.BlockSpec(memory_space=pltpu.VMEM)
+    copies = 27
+    return pl.pallas_call(
+        embed_kernel,
+        out_shape=jax.ShapeDtypeStruct((OWN, 1024), BF16),
+        in_specs=[vmem] * 9,
+        out_specs=vmem,
+        scratch_shapes=[
+            pltpu.VMEM((GROUP, PACK, 256), BF16),
+            pltpu.VMEM((GROUP, KMAX * CHAR_DIM, SLICE), BF16),
+            pltpu.VMEM((GROUP, 8, SLICE), F32),
+            pltpu.VMEM((8, 256, 128), BF16),
+            pltpu.VMEM((BLOCK, 512), BF16),
+            pltpu.VMEM((8, 256, WIDE), BF16),
+            pltpu.VMEM((BLOCK, WIDE), F32),
+            pltpu.VMEM((GROUP, BLOCK, WIDE), BF16),
+            pltpu.VMEM((BLOCK, WIDE), BF16),
+            pltpu.VMEM((GROUP, OWN, 1024), BF16),
+            pltpu.VMEM((GROUP - 1, OWN, 1024), BF16),
+            pltpu.SemaphoreType.DMA((copies,)),
+            pltpu.SemaphoreType.DMA((copies,)),
+        ],
+        compiler_params=pltpu.CompilerParams(
+            collective_id=0, has_side_effects=True, vmem_limit_bytes=56 << 20
+        ),
+        name="embed",
+    )(
+        char_ids, char_table, conv_weight, conv_bias.reshape(1, SLICE), hid, gate,
+        hid_bias.reshape(1, SLICE), gate_bias.reshape(1, SLICE), proj,
     )
-
-
-def char_features(char_ids, char_table, masked, conv_bias):
-    word_total = char_ids.shape[1]
-    blocks = char_ids.reshape(CHAR_LEN, 8, word_total // 8).transpose(1, 0, 2)
-
-    def conv_block(char_block):
-        windows = window_rows(char_table, char_block)
-        flat = windows.reshape(-1, KMAX * CHAR_DIM)
-        conv = jnp.dot(flat, masked, preferred_element_type=jnp.float32)
-        conv = conv.reshape(windows.shape[0], CHAR_LEN, masked.shape[1])
-        return jnp.tanh(jnp.max(conv, axis=1) + conv_bias).astype(jnp.bfloat16)
-
-    return lax.map(conv_block, blocks).reshape(word_total, masked.shape[1])
 
 
 def score_rows(work, work_targets, bound, embeddings, word_at, row_words, span_rows):
@@ -103,33 +279,13 @@
 ):
     word_at = lax.axis_index("word")
     tok_at = lax.axis_index("tok")
-    word_size = lax.axis_size("word")
-    filt_dev = conv_weight.shape[1]
-    masked = conv_weight * filter_mask(word_at * filt_dev, filt_dev).astype(jnp.bfloat16)
-    feats = char_features(char_ids, char_table, masked, conv_bias)
-    row_words = feats.shape[0]
-    weights_both = jnp.concatenate([highway_hid, highway_gate], axis=1)
-    mixed = jnp.dot(
-        lax.all_gather(feats, "word", axis=1, tiled=True),
-        weights_both,
-        preferred_element_type=jnp.float32,
-    )
-    hid_in = mixed[:, :filt_dev] + hid_bias
-    gate_in = mixed[:, filt_dev:] + gate_bias
-    opened = jax.nn.sigmoid(gate_in)
-    highway = (opened * jax.nn.relu(hid_in) + (1.0 - opened) * feats.astype(jnp.float32)).astype(
-        jnp.bfloat16
-    )
-    span_rows = row_words // word_size
-    embeddings = lax.psum_scatter(
-        jnp.dot(highway, proj_weight, preferred_element_type=jnp.float32).astype(jnp.bfloat16),
-        "word",
-        scatter_dimension=0,
-        tiled=True,
+    embeddings = build_embeddings(
+        char_ids, char_table, conv_weight, conv_bias, highway_hid, highway_gate, hid_bias, gate_bias,
+        proj_weight,
     )
     own_count = lax.dynamic_index_in_dim(counts, tok_at, keepdims=False)
     own_targets = lax.dynamic_slice_in_dim(targets, tok_at * TOK_DEV, TOK_DEV)
-    logprob = score_rows(hidden, own_targets, own_count, embeddings, word_at, row_words, span_rows)
+    logprob = score_rows(hidden, own_targets, own_count, embeddings, word_at, GROUP * BLOCK, OWN)
     return (embeddings, logprob)
 
 

time: 741 us -> 300 us (0.40)
  the two profiles are of different devices: /device:TPU:2 before, /device:TPU:34 now
where the time goes in v1:
time: 300 us; the launch traced here: 299 us
  waiting for transfers between devices  105 us (35%)
  blocking collectives  97.1 us (32%)
  Pallas kernels  52.4 us (17%)
  matrix products  21.2 us (7%)
  between operations  14.7 us (5%)
  other arithmetic  5.01 us (2%)
  local copies, waits for them, and re-layouts  3.68 us (1%)
    all_gather x1, waiting for transfers between devices, score_rows(): portion = lax.all_gather(embeddings, 'tok', axis=0, tiled=True)  105 us
    pmax x1, blocking collectives, score_rows(): top_score = lax.pmax(row_best, 'word')  54.6 us
    pallas_call x1, Pallas kernels, build_embeddings(): pl.pallas_call(embed_kernel, out_shape=jax.ShapeDtypeStruct((OWN, 1024),...  52.4 us
    psum x1, blocking collectives, score_rows(): lax.psum((row_total * jnp.exp(row_best - top_score), row_pick), 'word')  42.5 us
    dot_general x4, matrix products, one_block(): lax.dot_general(queries, portion, (((1,), (1,)), ((), ())), preferred_ele...  21.2 us
  transfers between devices with their start and end apart: 1, of which 1 were waited for; matrix products, arithmetic and copies ran while one was open for 1% of the time, Pallas kernels for 0%

profile of v1, /device:TPU:34, one launch (start us, length us, event | category | flops | bytes accessed | tf_op | source)
XLA Modules:
  0.0 299.2 jit_solution(4750038800609674716)
XLA Ops:
  7.2 0.0 all-gather.2.cloned.1.call-start
  7.2 1.4 copy.14.table_ref
  8.6 52.4 %embed.1 = bf16[104,1024]{1,0:T(8,128)(2,1)} custom-call(s32[24,1664]{1,0:T(8,128)} %ids_ref.1, bf16[256,16]{1,0:T(8,128)(2,1)} %copy.14.table_ref, bf16[112,128]{1,0:T(8,128)(2,1)} %conv_ref.1, f32[1,128]{1,0:T(1,128)} %bitcast.7, bf16[2048,128]{1,0:T(8,128)(2,1)} %hid_ref.1, bf16[2048,128]{1,0:T(8,128)(2,1)} %gate_ref.1, f32[1,128]{1,0:T(1,128)} %bitcast.8, ...), custom_call_target="tpu_custom_call" | custom-call | tf_op jit(solution)/shard_map/embed/pallas_call | solution.py:192
  61.1 0.0 all-gather.2.cloned.1.call-update
  61.1 1.2 dynamic_slice.22
  63.0 0.8 compare_select_fusion
  63.8 104.9 %all-gather.2.cloned.1.call-done = bf16[3328,1024]{1,0:T(8,128)(2,1)} async-done(((bf16[104,1024]{1,0:T(8,128)(2,1)}), bf16[3328,1024]{1,0:T(8,128)(2,1)}) %all-gather.2.cloned.1.call-update) | async-done | bytes 6815760 | tf_op jit(solution)/shard_map/all_gather | solution.py:233
  168.7 0.0 copy-start
  168.7 24.7 %while.15 = (s32[]{:T(128)}, f32[256]{0:T(256)S(1)}, f32[256]{0:T(256)S(1)}, f32[256]{0:T(256)S(1)}, s32[]{:T(128)}, /*index=5*/bf16[256,1024]{1,0:T(8,128)(2,1)...) while((s32[]{:T(128)}, f32[256]{0:T(256)S(1)}, ...), condition=%wide.region_4.5_spmd.clone, body=%wide.region_0.4_spmd.clone.sunk | while | flops 437485696 | bytes 8662963 | solution.py:258
  168.7 5.3 %fusion.13 = (f32[64]{0:T(128)S(1)}, f32[64,3328]{1,0:T(8,128)S(1)}) fusion(bf16[3328,1024]{1,0:T(8,128)(2,1)} %get-tuple-element.196, bf16[256,1024]{1,0:T(8,128)(2,1)} %get-tuple-element.195, s32[]{:T(128)S(6)} %select_n.88), kind=kOutput, calls=%fused_computation.19.clone.1 | convolution fusion | flops 436420544 | bytes 7799044 | tf_op jit(solution)/shard_map/while/body/dot_general | solution.py:240
  174.1 0.2 fusion.14
  174.3 0.1 dynamic_slice.44
  174.3 0.4 select_reduce_fusion.2
  174.7 0.2 add_dynamic-update-slice_fusion.3
  174.9 5.3 %fusion.13 = (f32[64]{0:T(128)S(1)}, f32[64,3328]{1,0:T(8,128)S(1)}) fusion(bf16[3328,1024]{1,0:T(8,128)(2,1)} %get-tuple-element.196, bf16[256,1024]{1,0:T(8,128)(2,1)} %get-tuple-element.195, s32[]{:T(128)S(6)} %select_n.88), kind=kOutput, calls=%fused_computation.19.clone.1 | convolution fusion | flops 436420544 | bytes 7799044 | tf_op jit(solution)/shard_map/while/body/dot_general | solution.py:240
  180.2 0.2 fusion.14
  180.4 0.1 dynamic_slice.44
  180.5 0.4 select_reduce_fusion.2
  180.9 0.2 add_dynamic-update-slice_fusion.3
  181.1 5.3 %fusion.13 = (f32[64]{0:T(128)S(1)}, f32[64,3328]{1,0:T(8,128)S(1)}) fusion(bf16[3328,1024]{1,0:T(8,128)(2,1)} %get-tuple-element.196, bf16[256,1024]{1,0:T(8,128)(2,1)} %get-tuple-element.195, s32[]{:T(128)S(6)} %select_n.88), kind=kOutput, calls=%fused_computation.19.clone.1 | convolution fusion | flops 436420544 | bytes 7799044 | tf_op jit(solution)/shard_map/while/body/dot_general | solution.py:240
  186.4 0.2 fusion.14
  186.6 0.1 dynamic_slice.44
  186.6 0.4 select_reduce_fusion.2
  187.0 0.2 add_dynamic-update-slice_fusion.3
  187.2 5.3 %fusion.13 = (f32[64]{0:T(128)S(1)}, f32[64,3328]{1,0:T(8,128)S(1)}) fusion(bf16[3328,1024]{1,0:T(8,128)(2,1)} %get-tuple-element.196, bf16[256,1024]{1,0:T(8,128)(2,1)} %get-tuple-element.195, s32[]{:T(128)S(6)} %select_n.88), kind=kOutput, calls=%fused_computation.19.clone.1 | convolution fusion | flops 436420544 | bytes 7799044 | tf_op jit(solution)/shard_map/while/body/dot_general | solution.py:240
  192.5 0.2 fusion.14
  192.7 0.1 dynamic_slice.44
  192.8 0.4 select_reduce_fusion.2
  193.2 0.2 add_dynamic-update-slice_fusion.3
  193.4 54.6 %pmax.7 = f32[256]{0:T(256)S(1)} all-reduce(f32[256]{0:T(256)S(1)} %get-tuple-element.53), channel_id=1, replica_groups=mesh['tok'=32,'word'=16] {'word'}, use_global_device_ids=true, to_apply=%region_6.7 | all-reduce | flops 256 | bytes 2048 | tf_op jit(solution)/shard_map/pmax | solution.py:259
  248.0 42.5 %all-reduce = (f32[256]{0:T(256)S(1)}, f32[256]{0:T(256)S(1)}) all-reduce(f32[256]{0:T(256)S(1)} %exponential_multiply_fusion, f32[256]{0:T(256)S(1)} %get-tuple-element.52), channel_id=1, replica_groups=mesh['tok'=32,'word'=16] {'word'}, use_global_device_ids=true, to_apply=%region_7.8 | all-reduce | flops 512 | bytes 4096 | tf_op jit(solution)/shard_map/psum | solution.py:260
  290.5 1.2 subtract_select_fusion
  291.7 0.0 copy-done
  291.7 0.7 copy.31
  (12 shorter events, 0.0 us)
Async XLA Ops:
  7.2 161.5 %all-gather.2.cloned.1.call-start = ((), (), s32[]{:S(2)}) async-start(), calls=%async_computation | async-start | bytes 7028736 | tf_op jit(solution)/shard_map/all_gather | solution.py:233
  168.7 123.0 %copy-start = (bf16[104,1024]{1,0:T(8,128)(2,1)S(1)}, bf16[104,1024]{1,0:T(8,128)(2,1)}, u32[]{:S(2)}) copy-start(bf16[104,1024]{1,0:T(8,128)(2,1)} %embed.1) | copy-start | bytes 638980
Sparse Core Ops, SparseCore 0:
  61.2 107.4 all-gather.1

commit v2 on v1

v2 whole, which is shorter than its diff:
```python
import functools

import jax
import jax.numpy as jnp
from jax import lax
from jax.experimental import pallas as pl
from jax.experimental.pallas import tpu as pltpu
from jax.sharding import PartitionSpec as P

CHAR_DIM = 16
KMAX = 7
CHAR_LEN = 24
FILTERS = 2048
TOK_DEV = 256
MESH = pl.DeviceIdType.MESH
BF16 = jnp.bfloat16
F32 = jnp.float32

GROUP = 4
OWN = 104
BLOCK = GROUP * OWN
SLICE = 128
WIDE = GROUP * SLICE
PACK = 2560
CHUNK = PACK // 8


def dot(a, b, contract=None, precision=None):
    if contract is None:
        return jnp.dot(a, b, preferred_element_type=F32, precision=precision)
    return lax.dot_general(a, b, (contract, ((), ())), preferred_element_type=F32)


def iota(shape, axis):
    return lax.broadcasted_iota(jnp.int32, shape, axis)


def one_hot(condition):
    return condition.astype(F32).astype(BF16)


COPIES = {
    "conv": 3, "bias": 3, "weight_z": 3, "weight_x": 9, "weight_core": 3, "feats": 3, "parts": 3,
    "row_z": 3, "row_zlo": 3, "row_y": 3, "emb_x": 3, "emb_core": 4, "stat_z": 3, "stat_zlo": 3, "stat_y": 3,
}
FIRST, TOTAL = {}, 0
for name, amount in COPIES.items():
    FIRST[name] = TOTAL
    TOTAL += amount


def merge_stats(pieces):
    top = pieces[0][0:1]
    for piece in pieces[1:]:
        top = jnp.maximum(top, piece[0:1])
    total = sum(piece[1:2] * jnp.exp(piece[0:1] - top) for piece in pieces)
    pick = sum(piece[2:3] for piece in pieces)
    return top, total, pick


def whole_kernel(
    counts_ref, ids_ref, table_ref, conv_ref, cbias_ref, hid_ref, gate_ref, hbias_ref, gbias_ref,
    proj_ref, hidden_ref, targets_ref,
    out_ref, logprob_ref,
    weights, convs, biases, tables, chars, shifted, best, feats, highway, parts, arrived,
    pieces, rows, words, scores, stat, zstat, lstat, ystat,
    send_sem, recv_sem,
):
    tok, word = lax.axis_index("tok"), lax.axis_index("word")
    zhi, x, core = tok // 8, (tok // 2) % 4, tok % 2
    y, zlo = word // 4, word % 4

    def at(zhi_to=zhi, x_to=x, core_to=core, y_to=y, zlo_to=zlo):
        return (zhi_to * 8 + x_to * 2 + core_to, y_to * 4 + zlo_to)

    sends = []

    def copy(name, index, src, dst, to):
        number = FIRST[name] + index
        return pltpu.make_async_remote_copy(
            src_ref=src, dst_ref=dst, send_sem=send_sem.at[number], recv_sem=recv_sem.at[number],
            device_id=to, device_id_type=MESH,
        )

    def start(name, index, src, dst, to):
        c = copy(name, index, src, dst, to)
        c.start()
        sends.append(c)

    def arrive(name, index, ref, to):
        copy(name, index, ref, ref, to).wait_recv()

    barrier = pltpu.get_barrier_semaphore()
    partners = [at(core_to=core ^ 1)]
    for d in (1, 2, 3):
        partners += [at(zlo_to=zlo ^ d), at(x_to=x ^ d), at(y_to=y ^ d), at(zhi_to=zhi ^ d)]
    for partner in partners:
        pl.semaphore_signal(barrier, inc=1, device_id=partner, device_id_type=MESH)

    convs[zlo] = conv_ref[...]
    biases[zlo, 0:1, :] = cbias_ref[...]
    biases[zlo, 1:2, :] = hbias_ref[...]
    biases[zlo, 2:3, :] = gbias_ref[...]
    weights[zlo, 0:2048, 0:128] = hid_ref[...]
    weights[zlo, 0:2048, 128:256] = gate_ref[...]
    for cb in range(4):
        weights[zlo, 2048 + cb * 128 : 2176 + cb * 128, :] = proj_ref[:, cb * 256 : cb * 256 + 256]
    place = word * 16 + iota((16, TOK_DEV), 0)
    place = jnp.where(zhi >= 2, TOK_DEV - 1 - place, place)
    pieces[zhi] = dot(one_hot(place == iota((16, TOK_DEV), 1)), hidden_ref[...]).astype(BF16)

    row = iota((BLOCK, 1), 0)
    block = (row >= OWN).astype(jnp.int32) + (row >= 2 * OWN).astype(jnp.int32) + (row >= 3 * OWN).astype(jnp.int32)
    source = row + block * (BLOCK - OWN) + zlo * OWN
    chosen = one_hot(source == iota((BLOCK, GROUP * BLOCK), 1))
    spelled = dot(chosen, ids_ref[...].astype(F32).astype(BF16), ((1,), (1,))).astype(jnp.int32)
    letter = iota((BLOCK, 256), 1)
    for j in range(8):
        shift = one_hot(iota((CHAR_DIM, 128), 1) == iota((CHAR_DIM, 128), 0) + CHAR_DIM * j)
        tables[j] = dot(table_ref[...], shift).astype(BF16)
    for i in range(3):
        total = jnp.zeros((BLOCK, 128), F32)
        for j in range(8):
            p = 8 * i + j
            total += dot(one_hot(spelled[:, p : p + 1] == letter), tables[j])
        chars[:, 128 * i : 128 * i + 128] = total.astype(BF16)
    chars[:, 384:512] = jnp.zeros((BLOCK, 128), BF16)

    pl.semaphore_wait(barrier, len(partners))

    mine = pl.ds(pl.multiple_of((core * 4 + x) * CHUNK, CHUNK), CHUNK)
    core_rows = pl.ds(pl.multiple_of(core * 4 * CHUNK, CHUNK), 4 * CHUNK)
    other_rows = pl.ds(pl.multiple_of((core ^ 1) * 4 * CHUNK, CHUNK), 4 * CHUNK)
    for d in (1, 2, 3):
        to = at(zlo_to=zlo ^ d)
        start("conv", d - 1, convs.at[zlo], convs.at[zlo], to)
        start("bias", d - 1, biases.at[zlo], biases.at[zlo], to)
    for d in (1, 2, 3):
        start("weight_z", d - 1, weights.at[zlo, mine], weights.at[zlo, mine], at(zlo_to=zlo ^ d))
    for d in (1, 2, 3):
        start("row_z", d - 1, pieces.at[zhi], pieces.at[zhi], at(zhi_to=zhi ^ d))

    for d in (1, 2, 3):
        arrive("conv", d - 1, convs.at[zlo ^ d], at(zlo_to=zlo ^ d))
        arrive("bias", d - 1, biases.at[zlo ^ d], at(zlo_to=zlo ^ d))
    tap = iota((KMAX * CHAR_DIM, WIDE), 0) >> 4
    number = y * WIDE + iota((KMAX * CHAR_DIM, WIDE), 1)
    keep = tap < 1 + ((number * KMAX) >> 11)
    filters = jnp.concatenate([convs[q] for q in range(GROUP)], axis=1).astype(F32)
    filters = jnp.where(keep, filters, 0.0).astype(BF16)
    for j in range(8):
        shifted[j] = jnp.zeros((256, WIDE), BF16)
        shifted[j, CHAR_DIM * j : CHAR_DIM * (j + KMAX), :] = filters
    best[...] = jnp.full((BLOCK, WIDE), -3e38, F32)

    def conv_step(j, carry):
        taps = shifted[j]
        top = dot(chars[:, 0:256], taps)
        top = jnp.maximum(top, dot(chars[:, 128:384], taps))
        top = jnp.maximum(top, dot(chars[:, 256:512], taps))
        best[...] = jnp.maximum(best[...], top)
        return carry

    lax.fori_loop(0, 8, conv_step, 0)
    bias = jnp.concatenate([biases[q, 0:1, :] for q in range(GROUP)], axis=1)
    feats[y] = jnp.tanh(best[...] + bias).astype(BF16)
    for d in (1, 2, 3):
        start("feats", d - 1, feats.at[y], feats.at[y], at(y_to=y ^ d))

    for d in (1, 2, 3):
        q = zlo ^ d
        arrive("weight_z", d - 1, weights.at[q, mine], at(zlo_to=q))
        for k in (1, 2, 3):
            start("weight_x", (d - 1) * 3 + k - 1, weights.at[q, mine], weights.at[q, mine], at(x_to=x ^ k))

    own_rows = pl.ds(pl.multiple_of(word * 16, 16), 16)
    y_rows = pl.ds(pl.multiple_of(y * 64, 64), 64)
    for d in (1, 2, 3):
        arrive("row_z", d - 1, pieces.at[zhi ^ d], at(zhi_to=zhi ^ d))
    position = word * 16 + iota((16, 1024), 0)
    for a in range(2):
        lower = position < counts_ref[a * 8 + x * 2 + core]
        rows[a, own_rows, :] = jnp.where(
            lower, pieces[a].astype(F32), pieces[a + 2].astype(F32)
        ).astype(BF16)
    for d in (1, 2, 3):
        start("row_zlo", d - 1, rows.at[:, own_rows], rows.at[:, own_rows], at(zlo_to=zlo ^ d))

    flip = one_hot(iota((TOK_DEV, TOK_DEV), 0) + iota((TOK_DEV, TOK_DEV), 1) == TOK_DEV - 1)
    lane = iota((1, TOK_DEV), 1)
    wanted = []
    for a in range(2):
        shard = a * 8 + x * 2 + core
        upper = targets_ref[pl.ds(shard + 16, 1), :]
        high, low = upper >> 8, upper & 255
        high = dot(high.astype(F32).astype(BF16), flip).astype(jnp.int32)
        low = dot(low.astype(F32).astype(BF16), flip).astype(jnp.int32)
        target = jnp.where(lane < counts_ref[shard], targets_ref[pl.ds(shard, 1), :], high * 256 + low)
        owner = target // (GROUP * BLOCK)
        rest = target - owner * (GROUP * BLOCK)
        slot = rest // OWN
        here = ((owner >> 3) == zhi) & (slot == word)
        local = (owner & 1) * BLOCK + ((owner >> 1) & 3) * OWN + rest - slot * OWN
        wanted.append(jnp.where(here, local, -1))
    wanted = jnp.concatenate(wanted, axis=1)

    for d in (1, 2, 3):
        q = zlo ^ d
        for k in (1, 2, 3):
            theirs = pl.ds(pl.multiple_of((core * 4 + (x ^ k)) * CHUNK, CHUNK), CHUNK)
            arrive("weight_x", (d - 1) * 3 + k - 1, weights.at[q, theirs], at(x_to=x ^ k))
        start("weight_core", d - 1, weights.at[q, core_rows], weights.at[q, core_rows], at(core_to=core ^ 1))
    for d in (1, 2, 3):
        arrive("weight_core", d - 1, weights.at[zlo ^ d, other_rows], at(core_to=core ^ 1))
    for d in (1, 2, 3):
        arrive("feats", d - 1, feats.at[y ^ d], at(y_to=y ^ d))

    for q in range(GROUP):
        mixed = dot(feats[0], weights[q, 0:512, :])
        for g in range(1, GROUP):
            mixed += dot(feats[g], weights[q, 512 * g : 512 * g + 512, :])
        hid_in = mixed[:, :128] + biases[q, 1:2, :]
        gate_in = mixed[:, 128:] + biases[q, 2:3, :]
        opened = jax.nn.sigmoid(gate_in)
        carried = feats[y, :, 128 * q : 128 * q + 128].astype(F32)
        highway[:, 128 * q : 128 * q + 128] = (
            opened * jnp.maximum(hid_in, 0.0) + (1.0 - opened) * carried
        ).astype(BF16)

    for cb in range(4):
        matrix = jnp.concatenate(
            [weights[q, 2048 + cb * 128 : 2176 + cb * 128, :] for q in range(GROUP)], axis=0
        )
        product = dot(highway[...], matrix)
        for g in range(GROUP):
            parts[g, :, cb * 256 : cb * 256 + 256] = product[g * OWN : g * OWN + OWN, :].astype(BF16)
    for d in (1, 2, 3):
        start("parts", d - 1, parts.at[y ^ d], arrived.at[d - 1], at(y_to=y ^ d))
    for d in (1, 2, 3):
        theirs = pl.ds(pl.multiple_of(y * 64 + (zlo ^ d) * 16, 16), 16)
        arrive("row_zlo", d - 1, rows.at[:, theirs], at(zlo_to=zlo ^ d))
    for d in (1, 2, 3):
        start("row_y", d - 1, rows.at[:, y_rows], rows.at[:, y_rows], at(y_to=y ^ d))
    total = parts[y].astype(F32)
    for d in (1, 2, 3):
        arrive("parts", d - 1, arrived.at[d - 1], at(y_to=y ^ d))
        total += arrived[d - 1].astype(F32)
    own_words = total.astype(BF16)
    out_ref[...] = own_words
    words[core, x] = own_words
    for k in (1, 2, 3):
        start("emb_x", k - 1, words.at[core, x], words.at[core, x], at(x_to=x ^ k))
    start("emb_core", 0, words.at[core, x], words.at[core, x], at(core_to=core ^ 1))
    for d in (1, 2, 3):
        theirs = pl.ds(pl.multiple_of((y ^ d) * 64, 64), 64)
        arrive("row_y", d - 1, rows.at[:, theirs], at(y_to=y ^ d))
    for k in (1, 2, 3):
        arrive("emb_x", k - 1, words.at[core, x ^ k], at(x_to=x ^ k))
        start("emb_core", k, words.at[core, x ^ k], words.at[core, x ^ k], at(core_to=core ^ 1))

    queries = rows[...].reshape(2 * TOK_DEV, 1024)

    def score(side):
        values = dot(words[side].reshape(BLOCK, 1024), queries, ((1,), (1,)))
        scores[...] = values
        values = scores[...]
        top = jnp.max(values, axis=0, keepdims=True)
        total = jnp.sum(jnp.exp(values - top), axis=0, keepdims=True)
        hits = iota((BLOCK, 2 * TOK_DEV), 0) == wanted - side * BLOCK
        pick = jnp.sum(jnp.where(hits, values, 0.0), axis=0, keepdims=True)
        return jnp.concatenate([top, total, pick], axis=0)

    near = score(core)
    arrive("emb_core", 0, words.at[core ^ 1, x], at(core_to=core ^ 1))
    for k in (1, 2, 3):
        arrive("emb_core", k, words.at[core ^ 1, x ^ k], at(core_to=core ^ 1))
    far = score(core ^ 1)

    def keep_stats(ref, at_rows, values):
        top, total, pick = values
        ref[at_rows + (slice(0, 1), slice(None))] = top
        ref[at_rows + (slice(1, 2), slice(None))] = total
        ref[at_rows + (slice(2, 3), slice(None))] = pick

    stat[...] = jnp.zeros((8, 2 * TOK_DEV), F32)
    keep_stats(stat, (), merge_stats([near, far]))

    def half(z):
        return pl.ds(pl.multiple_of((z % 2) * TOK_DEV, TOK_DEV), TOK_DEV)

    for d in (1, 2, 3):
        start("stat_z", d - 1, stat.at[:, half(zhi ^ d)], zstat.at[zhi], at(zhi_to=zhi ^ d))
    zstat[zhi] = stat[:, half(zhi)]
    for d in (1, 2, 3):
        arrive("stat_z", d - 1, zstat.at[zhi ^ d], at(zhi_to=zhi ^ d))
    lstat[zlo] = jnp.zeros((8, TOK_DEV), F32)
    keep_stats(lstat, (zlo,), merge_stats([zstat[n] for n in range(4)]))
    for d in (1, 2, 3):
        start("stat_zlo", d - 1, lstat.at[zlo], lstat.at[zlo], at(zlo_to=zlo ^ d))
    for d in (1, 2, 3):
        arrive("stat_zlo", d - 1, lstat.at[zlo ^ d], at(zlo_to=zlo ^ d))
    ystat[y] = jnp.zeros((8, TOK_DEV), F32)
    keep_stats(ystat, (y,), merge_stats([lstat[n] for n in range(4)]))
    for d in (1, 2, 3):
        start("stat_y", d - 1, ystat.at[y], ystat.at[y], at(y_to=y ^ d))
    for d in (1, 2, 3):
        arrive("stat_y", d - 1, ystat.at[y ^ d], at(y_to=y ^ d))
    top, total, pick = merge_stats([ystat[n] for n in range(4)])
    result = pick - (top + jnp.log(total))
    first = result.astype(BF16)
    left = result - first.astype(F32)
    second = left.astype(BF16)
    third = (left - second.astype(F32)).astype(BF16)
    turned = dot(first, flip) + dot(second, flip) + dot(third, flip)
    result = jnp.where(zhi >= 2, turned, result)
    logprob_ref[...] = jnp.where(lane < counts_ref[tok], result, 0.0)
    for c in sends:
        c.wait_send()


def on_device(
    char_ids,
    char_table,
    conv_weight,
    conv_bias,
    highway_hid,
    highway_gate,
    hid_bias,
    gate_bias,
    proj_weight,
    hidden,
    targets,
    counts,
):
    vmem = pl.BlockSpec(memory_space=pltpu.VMEM)
    embeddings, logprob = pl.pallas_call(
        whole_kernel,
        out_shape=(
            jax.ShapeDtypeStruct((OWN, 1024), BF16),
            jax.ShapeDtypeStruct((1, TOK_DEV), F32),
        ),
        in_specs=[pl.BlockSpec(memory_space=pltpu.SMEM)] + [vmem] * 11,
        out_specs=(vmem, vmem),
        scratch_shapes=[
            pltpu.VMEM((GROUP, PACK, 256), BF16),
            pltpu.VMEM((GROUP, KMAX * CHAR_DIM, SLICE), BF16),
            pltpu.VMEM((GROUP, 8, SLICE), F32),
            pltpu.VMEM((8, 256, 128), BF16),
            pltpu.VMEM((BLOCK, 512), BF16),
            pltpu.VMEM((8, 256, WIDE), BF16),
            pltpu.VMEM((BLOCK, WIDE), F32),
            pltpu.VMEM((GROUP, BLOCK, WIDE), BF16),
            pltpu.VMEM((BLOCK, WIDE), BF16),
            pltpu.VMEM((GROUP, OWN, 1024), BF16),
            pltpu.VMEM((GROUP - 1, OWN, 1024), BF16),
            pltpu.VMEM((4, 16, 1024), BF16),
            pltpu.VMEM((2, TOK_DEV, 1024), BF16),
            pltpu.VMEM((2, GROUP, OWN, 1024), BF16),
            pltpu.VMEM((BLOCK, 2 * TOK_DEV), F32),
            pltpu.VMEM((8, 2 * TOK_DEV), F32),
            pltpu.VMEM((4, 8, TOK_DEV), F32),
            pltpu.VMEM((4, 8, TOK_DEV), F32),
            pltpu.VMEM((4, 8, TOK_DEV), F32),
            pltpu.SemaphoreType.DMA((TOTAL,)),
            pltpu.SemaphoreType.DMA((TOTAL,)),
        ],
        compiler_params=pltpu.CompilerParams(
            collective_id=0, has_side_effects=True, vmem_limit_bytes=56 << 20
        ),
        name="whole",
    )(
        counts, char_ids, char_table, conv_weight, conv_bias.reshape(1, SLICE), highway_hid, highway_gate,
        hid_bias.reshape(1, SLICE), gate_bias.reshape(1, SLICE), proj_weight, hidden,
        targets.reshape(32, TOK_DEV),
    )
    return embeddings, logprob.reshape(TOK_DEV)


def solution(mesh):
    return jax.shard_map(
        on_device,
        mesh=mesh,
        in_specs=(
            P(None, "tok"),
            P(),
            P(None, "word"),
            P("word"),
            P(None, "word"),
            P(None, "word"),
            P("word"),
            P("word"),
            P("word", None),
            P("tok", None),
            P(),
            P(),
        ),
        out_specs=(P(("tok", "word"), None), P("tok")),
        check_vma=False,
    )
```

time: 300 us -> 99.2 us (0.33)
  the two profiles are of different devices: /device:TPU:34 before, /device:TPU:2 now
where the time goes in v2:
time: 99.2 us; the launch traced here: 98.7 us
  Pallas kernels  93.7 us (94%)
  local copies, waits for them, and re-layouts  4.31 us (4%)
    pallas_call x1, Pallas kernels, on_device(): pl.pallas_call(whole_kernel, out_shape=(jax.ShapeDtypeStruct((OWN, 1024),...  93.7 us
    unnamed x7, local copies, waits for them, and re-layouts  2.93 us

profile of v2, /device:TPU:2, one launch (start us, length us, event | category | flops | bytes accessed | tf_op | source)
XLA Modules:
  0.0 98.7 jit_solution(10370131589342743073)
XLA Ops:
  0.6 0.0 copy-start
  0.6 1.4 %reshape.22.targets_ref = s32[32,256]{1,0:T(8,128)} reshape(s32[8192]{0:T(1024)} %param.22) | data formatting | bytes 65536 | tf_op jit(solution)/shard_map/reshape | solution.py:374
  2.0 0.0 copy-done
  2.0 0.7 copy.14.table_ref
  2.7 93.7 %whole.1 = (bf16[104,1024]{1,0:T(8,128)(2,1)}, f32[1,256]{1,0:T(1,128)}) custom-call(s32[32]{0:T(128)} %counts_ref.1, s32[24,1664]{1,0:T(8,128)} %ids_ref.1, bf16[256,16]{1,0:T(8,128)(2,1)} %copy.14.table_ref, bf16[112,128]{1,0:T(8,128)(2,1)} %conv_ref.1, f32[1,128]{1,0:T(1,128)} %bitcast.5, bf16[2048,128]{1,0:T(8,128)(2,1)} %hid_ref.1, ...), custom_call_target="tpu_custom_call" | custom-call | tf_op jit(solution)/shard_map/whole/pallas_call | solution.py:336
  96.5 0.0 copy-start.1
  96.5 1.6 %copy.17 = bf16[104,1024]{1,0:T(8,128)(2,1)} copy(bf16[104,1024]{1,0:T(8,128)(2,1)} %get-tuple-element.8) | data formatting | bytes 425984
  98.1 0.0 copy-done.1
  98.1 0.6 copy.18
Async XLA Ops:
  0.6 1.4 %copy-start = (bf16[256,16]{0,1:T(8,128)(2,1)S(1)}, bf16[256,16]{0,1:T(8,128)(2,1)}, u32[]{:S(2)}) copy-start(bf16[256,16]{0,1:T(8,128)(2,1)} %param.13) | copy-start | bytes 24580
  96.5 1.6 %copy-start.1 = (f32[1,256]{1,0:T(1,128)S(1)}, f32[1,256]{1,0:T(1,128)}, u32[]{:S(2)}) copy-start(f32[1,256]{1,0:T(1,128)} %get-tuple-element.5) | copy-start | bytes 3076

commit v3 on v2

v3 whole, which is shorter than its diff:
```python
import functools

import jax
import jax.numpy as jnp
from jax import lax
from jax.experimental import pallas as pl
from jax.experimental.pallas import tpu as pltpu
from jax.sharding import PartitionSpec as P

CHAR_DIM = 16
KMAX = 7
CHAR_LEN = 24
FILTERS = 2048
TOK_DEV = 256
MESH = pl.DeviceIdType.MESH
BF16 = jnp.bfloat16
F32 = jnp.float32

GROUP = 4
OWN = 104
BLOCK = GROUP * OWN
SLICE = 128
WIDE = GROUP * SLICE
PACK = 2560
PIECE = PACK // 16
HALF = BLOCK // 2
CHUNKS = 2
WIDTH = 1024 // CHUNKS


def dot(a, b, contract=None, precision=None):
    if contract is None:
        return jnp.dot(a, b, preferred_element_type=F32, precision=precision)
    return lax.dot_general(a, b, (contract, ((), ())), preferred_element_type=F32)


def iota(shape, axis):
    return lax.broadcasted_iota(jnp.int32, shape, axis)


def one_hot(condition):
    return condition.astype(F32).astype(BF16)


COPIES = {
    "conv": 3, "bias": 3, "weight_z": 6, "weight_x": 12, "weight_far": 6, "weight_core": 6,
    "feats": 4, "feats_far": 2, "parts": 3 * CHUNKS, "row_z": 3, "row_zlo": 3, "row_y": 2, "row_far": 2,
    "emb_x": 2 * CHUNKS, "emb_far": CHUNKS, "emb_core": CHUNKS, "stat_z": 15, "stat_y": 3,
}
FIRST, TOTAL = {}, 0
for name, amount in COPIES.items():
    FIRST[name] = TOTAL
    TOTAL += amount


def merge_stats(pieces):
    half = pieces[0].shape[0] // 2
    top = pieces[0][:half]
    for piece in pieces[1:]:
        top = jnp.maximum(top, piece[:half])
    total = sum(jnp.exp(piece[:half] - top) for piece in pieces)
    pick = sum(piece[half:] for piece in pieces)
    return jnp.concatenate([top + jnp.log(total), pick], axis=0)


def whole_kernel(
    counts_ref, ids_ref, table_ref, conv_ref, cbias_ref, hid_ref, gate_ref, hbias_ref, gbias_ref,
    proj_ref, hidden_ref, targets_ref,
    out_ref, logprob_ref,
    weights, convs, biases, tables, chars, shifted, best, feats, highway, parts, arrived,
    pieces, rows, words, scores, stat, zstat, ystat,
    send_sem, recv_sem,
):
    tok, word = lax.axis_index("tok"), lax.axis_index("word")
    zhi, x, core = tok // 8, (tok // 2) % 4, tok % 2
    y, zlo = word // 4, word % 4

    def at(zhi_to=zhi, x_to=x, core_to=core, y_to=y, zlo_to=zlo):
        return (zhi_to * 8 + x_to * 2 + core_to, y_to * 4 + zlo_to)

    sends = []

    def copy(name, index, src, dst, to):
        number = FIRST[name] + index
        return pltpu.make_async_remote_copy(
            src_ref=src, dst_ref=dst, send_sem=send_sem.at[number], recv_sem=recv_sem.at[number],
            device_id=to, device_id_type=MESH,
        )

    def start(name, index, src, dst, to):
        c = copy(name, index, src, dst, to)
        c.start()
        sends.append(c)

    def arrive(name, index, ref, to):
        copy(name, index, ref, ref, to).wait_recv()

    barrier = pltpu.get_barrier_semaphore()
    partners = [at(core_to=core ^ 1)]
    for d in (1, 2, 3):
        partners += [at(x_to=x ^ d), at(y_to=y ^ d)]
    partners += [at(zhi_to=zhi ^ (d >> 2), zlo_to=zlo ^ (d & 3)) for d in range(1, 16)]
    for partner in partners:
        pl.semaphore_signal(barrier, inc=1, device_id=partner, device_id_type=MESH)

    convs[zlo] = conv_ref[...]
    biases[zlo, 0:1, :] = cbias_ref[...]
    biases[zlo, 1:2, :] = hbias_ref[...]
    biases[zlo, 2:3, :] = gbias_ref[...]
    weights[zlo, 0:2048, 0:128] = hid_ref[...]
    weights[zlo, 0:2048, 128:256] = gate_ref[...]
    for cb in range(4):
        weights[zlo, 2048 + cb * 128 : 2176 + cb * 128, :] = proj_ref[:, cb * 256 : cb * 256 + 256]
    place = word * 16 + iota((16, TOK_DEV), 0)
    place = jnp.where(zhi >= 2, TOK_DEV - 1 - place, place)
    pieces[zhi] = dot(one_hot(place == iota((16, TOK_DEV), 1)), hidden_ref[...]).astype(BF16)

    row = iota((BLOCK, 1), 0)
    block = (row >= OWN).astype(jnp.int32) + (row >= 2 * OWN).astype(jnp.int32) + (row >= 3 * OWN).astype(jnp.int32)
    source = row + block * (BLOCK - OWN) + zlo * OWN
    chosen = one_hot(source == iota((BLOCK, GROUP * BLOCK), 1))
    spelled = dot(chosen, ids_ref[...].astype(F32).astype(BF16), ((1,), (1,))).astype(jnp.int32)
    letter = iota((BLOCK, 256), 1)
    for j in range(8):
        shift = one_hot(iota((CHAR_DIM, 128), 1) == iota((CHAR_DIM, 128), 0) + CHAR_DIM * j)
        tables[j] = dot(table_ref[...], shift, ((0,), (0,))).astype(BF16)
    for i in range(3):
        total = jnp.zeros((BLOCK, 128), F32)
        for j in range(8):
            p = 8 * i + j
            total += dot(one_hot(spelled[:, p : p + 1] == letter), tables[j])
        chars[:, 128 * i : 128 * i + 128] = total.astype(BF16)
    chars[:, 384:512] = jnp.zeros((BLOCK, 128), BF16)

    pl.semaphore_wait(barrier, len(partners))

    x_next, x_last, x_far = (x + 1) % 4, (x + 3) % 4, (x + 2) % 4
    y_next, y_last, y_far = (y + 1) % 4, (y + 3) % 4, (y + 2) % 4

    def piece(part, x_of):
        return pl.ds(pl.multiple_of(part * (PACK // 2) + core * (4 * PIECE) + x_of * PIECE, PIECE), PIECE)

    def core_pieces(part, core_of):
        return pl.ds(pl.multiple_of(part * (PACK // 2) + core_of * (4 * PIECE), 4 * PIECE), 4 * PIECE)

    def start_weights(part):
        for d in (1, 2, 3):
            ref = weights.at[zlo, piece(part, x)]
            start("weight_z", part * 3 + d - 1, ref, ref, at(zlo_to=zlo ^ d))

    for d in (1, 2, 3):
        to = at(zlo_to=zlo ^ d)
        start("conv", d - 1, convs.at[zlo], convs.at[zlo], to)
        start("bias", d - 1, biases.at[zlo], biases.at[zlo], to)
    start_weights(0)
    start_weights(1)
    for d in (1, 2, 3):
        start("row_z", d - 1, pieces.at[zhi], pieces.at[zhi], at(zhi_to=zhi ^ d))

    for d in (1, 2, 3):
        arrive("conv", d - 1, convs.at[zlo ^ d], at(zlo_to=zlo ^ d))
        arrive("bias", d - 1, biases.at[zlo ^ d], at(zlo_to=zlo ^ d))
    tap = iota((KMAX * CHAR_DIM, WIDE), 0) >> 4
    number = y * WIDE + iota((KMAX * CHAR_DIM, WIDE), 1)
    keep = tap < 1 + ((number * KMAX) >> 11)
    filters = jnp.concatenate([convs[q] for q in range(GROUP)], axis=1).astype(F32)
    filters = jnp.where(keep, filters, 0.0).astype(BF16)
    for j in range(8):
        shifted[j] = jnp.zeros((256, WIDE), BF16)
        shifted[j, CHAR_DIM * j : CHAR_DIM * (j + KMAX), :] = filters
    best[...] = jnp.full((BLOCK, WIDE), -3e38, F32)

    bias = jnp.concatenate([biases[q, 0:1, :] for q in range(GROUP)], axis=1)
    for h in range(2):
        low, high = h * HALF, h * HALF + HALF

        def conv_step(j, carry):
            taps = shifted[j]
            top = dot(chars[low:high, 0:256], taps)
            top = jnp.maximum(top, dot(chars[low:high, 128:384], taps))
            top = jnp.maximum(top, dot(chars[low:high, 256:512], taps))
            best[low:high, :] = jnp.maximum(best[low:high, :], top)
            return carry

        lax.fori_loop(0, 8, conv_step, 0)
        feats[y, low:high, :] = jnp.tanh(best[low:high, :] + bias).astype(BF16)
        ref = feats.at[y, low:high]
        start("feats", h, ref, ref, at(y_to=y_next))
        start("feats", 2 + h, ref, ref, at(y_to=y_last))

    def weights_to_x(part):
        for d in (1, 2, 3):
            ref = weights.at[zlo ^ d, piece(part, x)]
            arrive("weight_z", part * 3 + d - 1, ref, at(zlo_to=zlo ^ d))
            start("weight_x", part * 6 + d - 1, ref, ref, at(x_to=x_next))
            start("weight_x", part * 6 + 2 + d, ref, ref, at(x_to=x_last))

    def weights_far(part):
        neighbour, other, base = ((x_last, x_next, 0), (x_next, x_last, 9))[part]
        for d in (1, 2, 3):
            ref = weights.at[zlo ^ d, piece(part, neighbour)]
            arrive("weight_x", base + d - 1, ref, at(x_to=neighbour))
            start("weight_far", part * 3 + d - 1, ref, ref, at(x_to=other))

    def feats_far(h):
        neighbour, other = ((y_last, y_next), (y_next, y_last))[h]
        ref = feats.at[neighbour, h * HALF : h * HALF + HALF]
        arrive("feats", 3 * h, ref, at(y_to=neighbour))
        start("feats_far", h, ref, ref, at(y_to=other))

    weights_to_x(0)
    feats_far(0)
    weights_to_x(1)
    feats_far(1)
    weights_far(0)
    weights_far(1)

    own_rows = pl.ds(pl.multiple_of(word * 16, 16), 16)

    def y_rows(y_of):
        return pl.ds(pl.multiple_of(y_of * 64, 64), 64)

    for d in (1, 2, 3):
        arrive("row_z", d - 1, pieces.at[zhi ^ d], at(zhi_to=zhi ^ d))
    position = word * 16 + iota((16, 1024), 0)
    for a in range(2):
        lower = position < counts_ref[a * 8 + x * 2 + core]
        rows[a, own_rows, :] = jnp.where(
            lower, pieces[a].astype(F32), pieces[a + 2].astype(F32)
        ).astype(BF16)
    for d in (1, 2, 3):
        start("row_zlo", d - 1, rows.at[:, own_rows], rows.at[:, own_rows], at(zlo_to=zlo ^ d))

    flip = one_hot(iota((TOK_DEV, TOK_DEV), 0) + iota((TOK_DEV, TOK_DEV), 1) == TOK_DEV - 1)
    lane = iota((1, TOK_DEV), 1)

    def shard_targets(shard):
        both = targets_ref[pl.ds(2 * shard, 2), :]
        return jnp.concatenate([both[0:1, :], both[1:2, :]], axis=1)

    wanted = []
    for a in range(2):
        shard = a * 8 + x * 2 + core
        upper = shard_targets(shard + 16)
        high, low = upper >> 8, upper & 255
        high = dot(high.astype(F32).astype(BF16), flip).astype(jnp.int32)
        low = dot(low.astype(F32).astype(BF16), flip).astype(jnp.int32)
        target = jnp.where(lane < counts_ref[shard], shard_targets(shard), high * 256 + low)
        owner = target // (GROUP * BLOCK)
        rest = target - owner * (GROUP * BLOCK)
        slot = rest // OWN
        here = ((owner >> 3) == zhi) & (slot == word)
        local = ((owner & 1) ^ core) * BLOCK + ((owner >> 1) & 3) * OWN + rest - slot * OWN
        wanted.append(jnp.where(here, local, -1))
    wanted = jnp.concatenate(wanted, axis=1)

    for d in (1, 2, 3):
        theirs = pl.ds(pl.multiple_of(y * 64 + (zlo ^ d) * 16, 16), 16)
        arrive("row_zlo", d - 1, rows.at[:, theirs], at(zlo_to=zlo ^ d))
    ref = rows.at[:, y_rows(y)]
    start("row_y", 0, ref, ref, at(y_to=y_next))
    start("row_y", 1, ref, ref, at(y_to=y_last))

    for part, neighbour, base in ((0, x_next, 3), (1, x_last, 6)):
        for d in (1, 2, 3):
            q = zlo ^ d
            arrive("weight_x", base + d - 1, weights.at[q, piece(part, neighbour)], at(x_to=neighbour))
            arrive("weight_far", part * 3 + d - 1, weights.at[q, piece(part, x_far)], at(x_to=neighbour))
            ref = weights.at[q, core_pieces(part, core)]
            start("weight_core", part * 3 + d - 1, ref, ref, at(core_to=core ^ 1))
    arrive("feats", 1, feats.at[y_last, HALF:BLOCK], at(y_to=y_last))
    arrive("feats", 2, feats.at[y_next, 0:HALF], at(y_to=y_next))
    arrive("feats_far", 0, feats.at[y_far, 0:HALF], at(y_to=y_last))
    arrive("feats_far", 1, feats.at[y_far, HALF:BLOCK], at(y_to=y_next))

    for d in range(4):
        q = zlo ^ d
        if d:
            for part in range(2):
                ref = weights.at[q, core_pieces(part, core ^ 1)]
                arrive("weight_core", part * 3 + d - 1, ref, at(core_to=core ^ 1))
        mixed = dot(feats[0], weights[q, 0:512, :])
        for g in range(1, GROUP):
            mixed += dot(feats[g], weights[q, 512 * g : 512 * g + 512, :])
        hid_in = mixed[:, :128] + biases[q, 1:2, :]
        gate_in = mixed[:, 128:] + biases[q, 2:3, :]
        opened = jax.nn.sigmoid(gate_in)
        columns = pl.ds(pl.multiple_of(q * SLICE, SLICE), SLICE)
        carried = feats[y, :, columns].astype(F32)
        highway[:, columns] = (opened * jnp.maximum(hid_in, 0.0) + (1.0 - opened) * carried).astype(BF16)

    for c in range(CHUNKS):
        for cb in range(c * WIDTH // 256, (c + 1) * WIDTH // 256):
            matrix = jnp.concatenate(
                [weights[q, 2048 + cb * 128 : 2176 + cb * 128, :] for q in range(GROUP)], axis=0
            )
            product = dot(highway[...], matrix).astype(BF16)
            column = cb * 256 - c * WIDTH
            for g in range(GROUP):
                parts[c, g, :, column : column + 256] = product[g * OWN : g * OWN + OWN, :]
        for d in (1, 2, 3):
            start("parts", 3 * c + d - 1, parts.at[c, y ^ d], arrived.at[c, d - 1], at(y_to=y ^ d))

    arrive("row_y", 0, rows.at[:, y_rows(y_last)], at(y_to=y_last))
    ref = rows.at[0, y_rows(y_last)]
    start("row_far", 0, ref, ref, at(y_to=y_next))
    arrive("row_y", 1, rows.at[:, y_rows(y_next)], at(y_to=y_next))
    ref = rows.at[1, y_rows(y_next)]
    start("row_far", 1, ref, ref, at(y_to=y_last))

    def sum_chunk(c):
        total = parts[c, y].astype(F32)
        for d in (1, 2, 3):
            arrive("parts", 3 * c + d - 1, arrived.at[c, d - 1], at(y_to=y ^ d))
            total += arrived[c, d - 1].astype(F32)
        own_words = total.astype(BF16)
        out_ref[:, c * WIDTH : c * WIDTH + WIDTH] = own_words
        words[core, c, x] = own_words
        ref = words.at[core, c, x]
        start("emb_x", 2 * c, ref, ref, at(x_to=x_next))
        start("emb_x", 2 * c + 1, ref, ref, at(x_to=x_last))

    def forward_chunk(c):
        arrive("emb_x", 2 * c, words.at[core, c, x_last], at(x_to=x_last))
        if c % 2 == 0:
            ref = words.at[core, c, x_last]
            start("emb_far", c, ref, ref, at(x_to=x_next))
        arrive("emb_x", 2 * c + 1, words.at[core, c, x_next], at(x_to=x_next))
        if c % 2 == 1:
            ref = words.at[core, c, x_next]
            start("emb_far", c, ref, ref, at(x_to=x_last))

    def share_chunk(c):
        arrive("emb_far", c, words.at[core, c, x_far], at(x_to=x_last if c % 2 == 0 else x_next))
        start("emb_core", c, words.at[core, c], words.at[core, c], at(core_to=core ^ 1))

    def score_side(c, side):
        queries = rows[:, :, c * WIDTH : c * WIDTH + WIDTH].reshape(2 * TOK_DEV, WIDTH)
        values = dot(words[core ^ side, c].reshape(BLOCK, WIDTH), queries, ((1,), (1,)))
        scores[side] = values if c == 0 else scores[side] + values

    def score_chunk(c):
        if c == 0:
            arrive("row_far", 0, rows.at[0, y_rows(y_far)], at(y_to=y_last))
            arrive("row_far", 1, rows.at[1, y_rows(y_far)], at(y_to=y_next))
        score_side(c, 0)
        arrive("emb_core", c, words.at[core ^ 1, c], at(core_to=core ^ 1))
        score_side(c, 1)

    for step in range(CHUNKS + 4):
        for lag, action in ((0, sum_chunk), (2, forward_chunk), (3, share_chunk), (4, score_chunk)):
            if 0 <= step - lag < CHUNKS:
                action(step - lag)

    def statistics(side):
        values = scores[side]
        top = jnp.max(values, axis=0, keepdims=True)
        total = jnp.sum(jnp.exp(values - top), axis=0, keepdims=True)
        hits = iota((BLOCK, 2 * TOK_DEV), 0) == wanted - side * BLOCK
        pick = jnp.sum(jnp.where(hits, values, 0.0), axis=0, keepdims=True)
        return jnp.concatenate([top + jnp.log(total), pick], axis=0)

    both = merge_stats([statistics(0), statistics(1)])
    for a in range(2):
        for r in range(2):
            first = a * TOK_DEV + r * 128
            stat[a, r : r + 1, :] = both[0:1, first : first + 128]
            stat[a, r + 2 : r + 3, :] = both[1:2, first : first + 128]
    for d in range(1, 16):
        z_to = zhi ^ (d >> 2)
        start(
            "stat_z", d - 1, stat.at[z_to % 2], zstat.at[zhi * 4 + zlo],
            at(zhi_to=z_to, zlo_to=zlo ^ (d & 3)),
        )
    zstat[zhi * 4 + zlo] = stat[zhi % 2]
    for d in range(1, 16):
        z_of, l_of = zhi ^ (d >> 2), zlo ^ (d & 3)
        arrive("stat_z", d - 1, zstat.at[z_of * 4 + l_of], at(zhi_to=z_of, zlo_to=l_of))
    ystat[y] = merge_stats([zstat[n] for n in range(16)])
    for d in (1, 2, 3):
        start("stat_y", d - 1, ystat.at[y], ystat.at[y], at(y_to=y ^ d))
    for d in (1, 2, 3):
        arrive("stat_y", d - 1, ystat.at[y ^ d], at(y_to=y ^ d))
    both = merge_stats([ystat[n] for n in range(4)])
    result = both[2:4] - both[0:2]
    result = jnp.concatenate([result[0:1], result[1:2]], axis=1)
    first = result.astype(BF16)
    left = result - first.astype(F32)
    second = left.astype(BF16)
    third = (left - second.astype(F32)).astype(BF16)
    turned = dot(first, flip) + dot(second, flip) + dot(third, flip)
    result = jnp.where(zhi >= 2, turned, result)
    result = jnp.where(lane < counts_ref[tok], result, 0.0)
    logprob_ref[0:1, :] = result[:, 0:128]
    logprob_ref[1:2, :] = result[:, 128:256]
    for c in sends:
        c.wait_send()


def on_device(
    char_ids,
    char_table,
    conv_weight,
    conv_bias,
    highway_hid,
    highway_gate,
    hid_bias,
    gate_bias,
    proj_weight,
    hidden,
    targets,
    counts,
):
    vmem = pl.BlockSpec(memory_space=pltpu.VMEM)
    embeddings, logprob = pl.pallas_call(
        whole_kernel,
        out_shape=(
            jax.ShapeDtypeStruct((OWN, 1024), BF16),
            jax.ShapeDtypeStruct((2, TOK_DEV // 2), F32),
        ),
        in_specs=[pl.BlockSpec(memory_space=pltpu.SMEM)] + [vmem] * 11,
        out_specs=(vmem, vmem),
        scratch_shapes=[
            pltpu.VMEM((GROUP, PACK, 256), BF16),
            pltpu.VMEM((GROUP, KMAX * CHAR_DIM, SLICE), BF16),
            pltpu.VMEM((GROUP, 8, SLICE), F32),
            pltpu.VMEM((8, 256, 128), BF16),
            pltpu.VMEM((BLOCK, 512), BF16),
            pltpu.VMEM((8, 256, WIDE), BF16),
            pltpu.VMEM((BLOCK, WIDE), F32),
            pltpu.VMEM((GROUP, BLOCK, WIDE), BF16),
            pltpu.VMEM((BLOCK, WIDE), BF16),
            pltpu.VMEM((CHUNKS, GROUP, OWN, WIDTH), BF16),
            pltpu.VMEM((CHUNKS, GROUP - 1, OWN, WIDTH), BF16),
            pltpu.VMEM((4, 16, 1024), BF16),
            pltpu.VMEM((2, TOK_DEV, 1024), BF16),
            pltpu.VMEM((2, CHUNKS, GROUP, OWN, WIDTH), BF16),
            pltpu.VMEM((2, BLOCK, 2 * TOK_DEV), F32),
            pltpu.VMEM((2, 4, 128), F32),
            pltpu.VMEM((16, 4, 128), F32),
            pltpu.VMEM((4, 4, 128), F32),
            pltpu.SemaphoreType.DMA((TOTAL,)),
            pltpu.SemaphoreType.DMA((TOTAL,)),
        ],
        compiler_params=pltpu.CompilerParams(
            collective_id=0, has_side_effects=True, vmem_limit_bytes=56 << 20
        ),
        name="whole",
    )(
        counts, char_ids, char_table.T, conv_weight, conv_bias.reshape(1, SLICE), highway_hid, highway_gate,
        hid_bias.reshape(1, SLICE), gate_bias.reshape(1, SLICE), proj_weight, hidden,
        targets.reshape(64, TOK_DEV // 2),
    )
    return embeddings, logprob.reshape(TOK_DEV)


def solution(mesh):
    return jax.shard_map(
        on_device,
        mesh=mesh,
        in_specs=(
            P(None, "tok"),
            P(),
            P(None, "word"),
            P("word"),
            P(None, "word"),
            P(None, "word"),
            P("word"),
            P("word"),
            P("word", None),
            P("tok", None),
            P(),
            P(),
        ),
        out_specs=(P(("tok", "word"), None), P("tok")),
        check_vma=False,
    )
```

time: 99.2 us -> 93 us (0.938)
  the two profiles are of different devices: /device:TPU:2 before, /device:TPU:6 now
where the time goes in v3:
time: 93 us; the launch traced here: 92.9 us
  Pallas kernels  90 us (97%)
  local copies, waits for them, and re-layouts  2.2 us (2%)
    pallas_call x1, Pallas kernels, on_device(): pl.pallas_call(whole_kernel, out_shape=(jax.ShapeDtypeStruct((OWN, 1024),...  90 us
    unnamed x4, local copies, waits for them, and re-layouts  2.2 us

profile of v3, /device:TPU:6, one launch (start us, length us, event | category | flops | bytes accessed | tf_op | source)
XLA Modules:
  0.0 92.9 jit_solution(7349588607605660205)
XLA Ops:
  0.6 90.0 %whole.1 = (bf16[104,1024]{1,0:T(8,128)(2,1)}, f32[2,128]{1,0:T(2,128)}) custom-call(s32[32]{0:T(128)} %counts_ref.1, s32[24,1664]{1,0:T(8,128)} %ids_ref.1, bf16[16,256]{1,0:T(8,128)(2,1)} %bitcast.7, bf16[112,128]{1,0:T(8,128)(2,1)} %conv_ref.1, f32[1,128]{1,0:T(1,128)} %bitcast.9, bf16[2048,128]{1,0:T(8,128)(2,1)} %hid_ref.1, bf16[2048,128]{1,0:T(8,128)(2,1)} %gate_ref.1, ...), custom_call_target="tpu_custom_call" | custom-call | tf_op jit(solution)/shard_map/whole/pallas_call | solution.py:415
  90.7 0.0 copy-start
  90.7 1.6 %copy.16 = bf16[104,1024]{1,0:T(8,128)(2,1)} copy(bf16[104,1024]{1,0:T(8,128)(2,1)} %get-tuple-element.8) | data formatting | bytes 425984
  92.3 0.0 copy-done
  92.3 0.6 copy.17
Async XLA Ops:
  90.7 1.6 %copy-start = (f32[2,128]{1,0:T(2,128)S(1)}, f32[2,128]{1,0:T(2,128)}, u32[]{:S(2)}) copy-start(f32[2,128]{1,0:T(2,128)} %get-tuple-element.5) | copy-start | bytes 3076

commit v4 on v3

--- a/solution.py
+++ b/solution.py
@@ -45,7 +45,7 @@
 COPIES = {
     "conv": 3, "bias": 3, "weight_z": 6, "weight_x": 12, "weight_far": 6, "weight_core": 6,
     "feats": 4, "feats_far": 2, "parts": 3 * CHUNKS, "row_z": 3, "row_zlo": 3, "row_y": 2, "row_far": 2,
-    "emb_x": 2 * CHUNKS, "emb_far": CHUNKS, "emb_core": CHUNKS, "stat_z": 15, "stat_y": 3,
+    "emb_x": 3 * CHUNKS, "emb_core": 4 * CHUNKS, "stat_z": 15, "stat_y": 3,
 }
 FIRST, TOTAL = {}, 0
 for name, amount in COPIES.items():
@@ -212,8 +212,6 @@
     feats_far(0)
     weights_to_x(1)
     feats_far(1)
-    weights_far(0)
-    weights_far(1)
 
     own_rows = pl.ds(pl.multiple_of(word * 16, 16), 16)
 
@@ -230,6 +228,9 @@
         ).astype(BF16)
     for d in (1, 2, 3):
         start("row_zlo", d - 1, rows.at[:, own_rows], rows.at[:, own_rows], at(zlo_to=zlo ^ d))
+
+    weights_far(0)
+    weights_far(1)
 
     flip = one_hot(iota((TOK_DEV, TOK_DEV), 0) + iota((TOK_DEV, TOK_DEV), 1) == TOK_DEV - 1)
     lane = iota((1, TOK_DEV), 1)
@@ -254,6 +255,13 @@
         wanted.append(jnp.where(here, local, -1))
     wanted = jnp.concatenate(wanted, axis=1)
 
+    for part, neighbour, base in ((0, x_next, 3), (1, x_last, 6)):
+        for d in (1, 2, 3):
+            q = zlo ^ d
+            arrive("weight_x", base + d - 1, weights.at[q, piece(part, neighbour)], at(x_to=neighbour))
+            arrive("weight_far", part * 3 + d - 1, weights.at[q, piece(part, x_far)], at(x_to=neighbour))
+            ref = weights.at[q, core_pieces(part, core)]
+            start("weight_core", part * 3 + d - 1, ref, ref, at(core_to=core ^ 1))
     for d in (1, 2, 3):
         theirs = pl.ds(pl.multiple_of(y * 64 + (zlo ^ d) * 16, 16), 16)
         arrive("row_zlo", d - 1, rows.at[:, theirs], at(zlo_to=zlo ^ d))
@@ -261,13 +269,6 @@
     start("row_y", 0, ref, ref, at(y_to=y_next))
     start("row_y", 1, ref, ref, at(y_to=y_last))
 
-    for part, neighbour, base in ((0, x_next, 3), (1, x_last, 6)):
-        for d in (1, 2, 3):
-            q = zlo ^ d
-            arrive("weight_x", base + d - 1, weights.at[q, piece(part, neighbour)], at(x_to=neighbour))
-            arrive("weight_far", part * 3 + d - 1, weights.at[q, piece(part, x_far)], at(x_to=neighbour))
-            ref = weights.at[q, core_pieces(part, core)]
-            start("weight_core", part * 3 + d - 1, ref, ref, at(core_to=core ^ 1))
     arrive("feats", 1, feats.at[y_last, HALF:BLOCK], at(y_to=y_last))
     arrive("feats", 2, feats.at[y_next, 0:HALF], at(y_to=y_next))
     arrive("feats_far", 0, feats.at[y_far, 0:HALF], at(y_to=y_last))
@@ -317,40 +318,22 @@
         out_ref[:, c * WIDTH : c * WIDTH + WIDTH] = own_words
         words[core, c, x] = own_words
         ref = words.at[core, c, x]
-        start("emb_x", 2 * c, ref, ref, at(x_to=x_next))
-        start("emb_x", 2 * c + 1, ref, ref, at(x_to=x_last))
-
-    def forward_chunk(c):
-        arrive("emb_x", 2 * c, words.at[core, c, x_last], at(x_to=x_last))
-        if c % 2 == 0:
-            ref = words.at[core, c, x_last]
-            start("emb_far", c, ref, ref, at(x_to=x_next))
-        arrive("emb_x", 2 * c + 1, words.at[core, c, x_next], at(x_to=x_next))
-        if c % 2 == 1:
-            ref = words.at[core, c, x_next]
-            start("emb_far", c, ref, ref, at(x_to=x_last))
+        for k in (2, 1, 3):
+            start("emb_x", 3 * c + k - 1, ref, ref, at(x_to=x ^ k))
+        start("emb_core", 4 * c, ref, ref, at(core_to=core ^ 1))
 
     def share_chunk(c):
-        arrive("emb_far", c, words.at[core, c, x_far], at(x_to=x_last if c % 2 == 0 else x_next))
-        start("emb_core", c, words.at[core, c], words.at[core, c], at(core_to=core ^ 1))
+        for k in (1, 3, 2):
+            ref = words.at[core, c, x ^ k]
+            arrive("emb_x", 3 * c + k - 1, ref, at(x_to=x ^ k))
+            start("emb_core", 4 * c + k, ref, ref, at(core_to=core ^ 1))
 
     def score_side(c, side):
         queries = rows[:, :, c * WIDTH : c * WIDTH + WIDTH].reshape(2 * TOK_DEV, WIDTH)
         values = dot(words[core ^ side, c].reshape(BLOCK, WIDTH), queries, ((1,), (1,)))
         scores[side] = values if c == 0 else scores[side] + values
 
-    def score_chunk(c):
-        if c == 0:
-            arrive("row_far", 0, rows.at[0, y_rows(y_far)], at(y_to=y_last))
-            arrive("row_far", 1, rows.at[1, y_rows(y_far)], at(y_to=y_next))
-        score_side(c, 0)
-        arrive("emb_core", c, words.at[core ^ 1, c], at(core_to=core ^ 1))
-        score_side(c, 1)
-
-    for step in range(CHUNKS + 4):
-        for lag, action in ((0, sum_chunk), (2, forward_chunk), (3, share_chunk), (4, score_chunk)):
-            if 0 <= step - lag < CHUNKS:
-                action(step - lag)
+    found = []
 
     def statistics(side):
         values = scores[side]
@@ -360,7 +343,23 @@
         pick = jnp.sum(jnp.where(hits, values, 0.0), axis=0, keepdims=True)
         return jnp.concatenate([top + jnp.log(total), pick], axis=0)
 
-    both = merge_stats([statistics(0), statistics(1)])
+    def score_chunk(c):
+        if c == 0:
+            arrive("row_far", 0, rows.at[0, y_rows(y_far)], at(y_to=y_last))
+            arrive("row_far", 1, rows.at[1, y_rows(y_far)], at(y_to=y_next))
+        score_side(c, 0)
+        if c == CHUNKS - 1:
+            found.append(statistics(0))
+        for k in range(4):
+            arrive("emb_core", 4 * c + k, words.at[core ^ 1, c, x ^ k], at(core_to=core ^ 1))
+        score_side(c, 1)
+
+    for step in range(CHUNKS + 2):
+        for lag, action in ((0, sum_chunk), (2, score_chunk), (1, share_chunk)):
+            if 0 <= step - lag < CHUNKS:
+                action(step - lag)
+
+    both = merge_stats([found[0], statistics(1)])
     for a in range(2):
         for r in range(2):
             first = a * TOK_DEV + r * 128

time: 93 us -> 91 us (0.978)
  the two profiles are of different devices: /device:TPU:6 before, /device:TPU:2 now
where the time goes in v4:
time: 91 us; the launch traced here: 90.8 us
  Pallas kernels  88 us (97%)
  local copies, waits for them, and re-layouts  2.2 us (2%)
    pallas_call x1, Pallas kernels, on_device(): pl.pallas_call(whole_kernel, out_shape=(jax.ShapeDtypeStruct((OWN, 1024),...  88 us
    unnamed x4, local copies, waits for them, and re-layouts  2.2 us

profile of v4, /device:TPU:2, one launch (start us, length us, event | category | flops | bytes accessed | tf_op | source)
XLA Modules:
  0.0 90.8 jit_solution(551626814884758124)
XLA Ops:
  0.6 88.0 %whole.1 = (bf16[104,1024]{1,0:T(8,128)(2,1)}, f32[2,128]{1,0:T(2,128)}) custom-call(s32[32]{0:T(128)} %counts_ref.1, s32[24,1664]{1,0:T(8,128)} %ids_ref.1, bf16[16,256]{1,0:T(8,128)(2,1)} %bitcast.7, bf16[112,128]{1,0:T(8,128)(2,1)} %conv_ref.1, f32[1,128]{1,0:T(1,128)} %bitcast.9, bf16[2048,128]{1,0:T(8,128)(2,1)} %hid_ref.1, bf16[2048,128]{1,0:T(8,128)(2,1)} %gate_ref.1, ...), custom_call_target="tpu_custom_call" | custom-call | tf_op jit(solution)/shard_map/whole/pallas_call | solution.py:414
  88.6 0.0 copy-start
  88.6 1.6 %copy.16 = bf16[104,1024]{1,0:T(8,128)(2,1)} copy(bf16[104,1024]{1,0:T(8,128)(2,1)} %get-tuple-element.8) | data formatting | bytes 425984
  90.3 0.0 copy-done
  90.3 0.6 copy.17
Async XLA Ops:
  88.6 1.6 %copy-start = (f32[2,128]{1,0:T(2,128)S(1)}, f32[2,128]{1,0:T(2,128)}, u32[]{:S(2)}) copy-start(f32[2,128]{1,0:T(2,128)} %get-tuple-element.5) | copy-start | bytes 3076

commit v5 on v4

--- a/solution.py
+++ b/solution.py
@@ -47,6 +47,7 @@
     "feats": 4, "feats_far": 2, "parts": 3 * CHUNKS, "row_z": 3, "row_zlo": 3, "row_y": 2, "row_far": 2,
     "emb_x": 3 * CHUNKS, "emb_core": 4 * CHUNKS, "stat_z": 15, "stat_y": 3,
 }
+FAR_FIRST = (8, 9, 10, 11, 4, 5, 6, 7, 12, 13, 14, 15, 3, 2, 1)
 FIRST, TOTAL = {}, 0
 for name, amount in COPIES.items():
     FIRST[name] = TOTAL
@@ -96,10 +97,10 @@
         copy(name, index, ref, ref, to).wait_recv()
 
     barrier = pltpu.get_barrier_semaphore()
-    partners = [at(core_to=core ^ 1)]
-    for d in (1, 2, 3):
+    partners = [at(zhi_to=zhi ^ (d >> 2), zlo_to=zlo ^ (d & 3)) for d in FAR_FIRST]
+    for d in (2, 1, 3):
         partners += [at(x_to=x ^ d), at(y_to=y ^ d)]
-    partners += [at(zhi_to=zhi ^ (d >> 2), zlo_to=zlo ^ (d & 3)) for d in range(1, 16)]
+    partners.append(at(core_to=core ^ 1))
     for partner in partners:
         pl.semaphore_signal(barrier, inc=1, device_id=partner, device_id_type=MESH)
 
@@ -154,7 +155,7 @@
         start("bias", d - 1, biases.at[zlo], biases.at[zlo], to)
     start_weights(0)
     start_weights(1)
-    for d in (1, 2, 3):
+    for d in (2, 1, 3):
         start("row_z", d - 1, pieces.at[zhi], pieces.at[zhi], at(zhi_to=zhi ^ d))
 
     for d in (1, 2, 3):
@@ -299,7 +300,7 @@
             column = cb * 256 - c * WIDTH
             for g in range(GROUP):
                 parts[c, g, :, column : column + 256] = product[g * OWN : g * OWN + OWN, :]
-        for d in (1, 2, 3):
+        for d in (2, 1, 3):
             start("parts", 3 * c + d - 1, parts.at[c, y ^ d], arrived.at[c, d - 1], at(y_to=y ^ d))
 
     arrive("row_y", 0, rows.at[:, y_rows(y_last)], at(y_to=y_last))
@@ -365,7 +366,7 @@
             first = a * TOK_DEV + r * 128
             stat[a, r : r + 1, :] = both[0:1, first : first + 128]
             stat[a, r + 2 : r + 3, :] = both[1:2, first : first + 128]
-    for d in range(1, 16):
+    for d in FAR_FIRST:
         z_to = zhi ^ (d >> 2)
         start(
             "stat_z", d - 1, stat.at[z_to % 2], zstat.at[zhi * 4 + zlo],
@@ -376,7 +377,7 @@
         z_of, l_of = zhi ^ (d >> 2), zlo ^ (d & 3)
         arrive("stat_z", d - 1, zstat.at[z_of * 4 + l_of], at(zhi_to=z_of, zlo_to=l_of))
     ystat[y] = merge_stats([zstat[n] for n in range(16)])
-    for d in (1, 2, 3):
+    for d in (2, 1, 3):
         start("stat_y", d - 1, ystat.at[y], ystat.at[y], at(y_to=y ^ d))
     for d in (1, 2, 3):
         arrive("stat_y", d - 1, ystat.at[y ^ d], at(y_to=y ^ d))

time: 91 us -> 90.9 us (level)
  no operation moved by 1% of the time
where the time goes in v5:
time: 90.9 us; the launch traced here: 90.7 us
  Pallas kernels  87.9 us (97%)
  local copies, waits for them, and re-layouts  2.2 us (2%)
    pallas_call x1, Pallas kernels, on_device(): pl.pallas_call(whole_kernel, out_shape=(jax.ShapeDtypeStruct((OWN, 1024),...  87.9 us
    unnamed x4, local copies, waits for them, and re-layouts  2.2 us

profile of v5, /device:TPU:2, one launch (start us, length us, event | category | flops | bytes accessed | tf_op | source)
XLA Modules:
  0.0 90.7 jit_solution(13682013345452054940)
XLA Ops:
  0.6 87.9 %whole.1 = (bf16[104,1024]{1,0:T(8,128)(2,1)}, f32[2,128]{1,0:T(2,128)}) custom-call(s32[32]{0:T(128)} %counts_ref.1, s32[24,1664]{1,0:T(8,128)} %ids_ref.1, bf16[16,256]{1,0:T(8,128)(2,1)} %bitcast.7, bf16[112,128]{1,0:T(8,128)(2,1)} %conv_ref.1, f32[1,128]{1,0:T(1,128)} %bitcast.9, bf16[2048,128]{1,0:T(8,128)(2,1)} %hid_ref.1, bf16[2048,128]{1,0:T(8,128)(2,1)} %gate_ref.1, ...), custom_call_target="tpu_custom_call" | custom-call | tf_op jit(solution)/shard_map/whole/pallas_call | solution.py:415
  88.5 0.0 copy-start
  88.5 1.6 %copy.16 = bf16[104,1024]{1,0:T(8,128)(2,1)} copy(bf16[104,1024]{1,0:T(8,128)(2,1)} %get-tuple-element.8) | data formatting | bytes 425984
  90.2 0.0 copy-done
  90.2 0.6 copy.17
Async XLA Ops:
  88.5 1.6 %copy-start = (f32[2,128]{1,0:T(2,128)S(1)}, f32[2,128]{1,0:T(2,128)}, u32[]{:S(2)}) copy-start(f32[2,128]{1,0:T(2,128)} %get-tuple-element.5) | copy-start | bytes 3076
